TPU v7x, 128 devices: a whole 4x4x4 slice. The times are simulated.
128 devices in a mesh: shard: 32 (over y, x, core), replica: 4 (over z).
Axes of the slice: x: 4, y: 4, z: 4, core: 2. Of those that a mesh axis runs over, the one named last changes fastest.
Arguments:
- tokens: bfloat16 [32768, 768], P(('shard', 'replica')), may hold values from -6 to 6
- cotangent: bfloat16 [32768, 768], P(('shard', 'replica')), may hold values from -6 to 6
- w_qkv: bfloat16 [768, 2304], P('shard'), may hold values from -0.21875 to 0.21875
- b_qkv: bfloat16 [2304], P('shard'), may hold values from -1.796875 to 1.796875
- w_out: bfloat16 [768, 768], P('shard'), may hold values from -0.875 to 0.875
- b_out: bfloat16 [768], P('shard'), may hold values from -1.796875 to 1.796875
- w_up: bfloat16 [768, 3072], P('shard'), may hold values from -0.21875 to 0.21875
- b_up: bfloat16 [3072], P('shard'), may hold values from -1.796875 to 1.796875
- w_down: bfloat16 [3072, 768], P('shard'), may hold values from -0.15625 to 0.15625
- b_down: bfloat16 [768], P('shard'), may hold values from -1.796875 to 1.796875
- ln1_gain: bfloat16 [768], P('shard'), may hold values from 0.5 to 1.5
- ln1_bias: bfloat16 [768], P('shard'), may hold values from -1.1953125 to 1.1953125
- ln2_gain: bfloat16 [768], P('shard'), may hold values from 0.5 to 1.5
- ln2_bias: bfloat16 [768], P('shard'), may hold values from -1.1953125 to 1.1953125
- seq_device: int32 [256], replicated, may hold values from 0 to 127, as said below
- seq_lengths: int32 [256], replicated, may hold values from 1 to 224, as said below
- seq_offsets: int32 [256], replicated, may hold values from 0 to 255, as said below
Outputs:
- mixed: bfloat16 [32768, 768], P(('shard', 'replica'))
- grad_tokens: bfloat16 [32768, 768], P(('shard', 'replica'))
- grad_w_qkv: float32 [768, 2304], P('shard')
- grad_b_qkv: float32 [2304], P('shard')
- grad_w_out: float32 [768, 768], P('shard')
- grad_b_out: float32 [768], P('shard')
- grad_w_up: float32 [768, 3072], P('shard')
- grad_b_up: float32 [3072], P('shard')
- grad_w_down: float32 [3072, 768], P('shard')
- grad_b_down: float32 [768], P('shard')
- grad_ln1_gain: float32 [768], P('shard')
- grad_ln1_bias: float32 [768], P('shard')
- grad_ln2_gain: float32 [768], P('shard')
- grad_ln2_bias: float32 [768], P('shard')
Inputs may be any that keep to these rules, and one draw needn't show every extreme that they name: `seq_device`: every device holds exactly two sequences. `seq_lengths`: some sequence in every draw has exactly 256 - 256 // 8 tokens. `seq_offsets`: A device's two sequences lie in its 256 slots without intersection and hold at most 256 tokens together; in every draw some device's two hold exactly 256.
All inputs are finite; a program needn't handle non-finite values.
Results may differ from a plain program's by a relative error of at most 0.023.
Values may be sent and summed in bfloat16 or wider, within the bound.
A program may use at most 128 MiB of HBM per device.

v0:
```python
import jax
import jax.numpy as jnp
from jax import lax
from jax.sharding import PartitionSpec as P

HD = 64
ROT = 16


EPS = 1e-05
INV_ROOT_TWO = 0.7071067811865476
INV_ROOT_TWO_PI = 0.3989422804014327


def norm_rows(x, gain, bias):
    mean = jnp.mean(x, axis=-1, keepdims=True)
    centered = x - mean
    var = jnp.mean(centered * centered, axis=-1, keepdims=True)
    inverse = lax.rsqrt(var + EPS)
    normal = centered * inverse
    return (normal * gain + bias, normal, inverse)


def norm_back(upstream, normal, inverse, gain):
    scaled = upstream * gain
    centre = jnp.mean(scaled, axis=-1, keepdims=True)
    slope = jnp.mean(scaled * normal, axis=-1, keepdims=True)
    return (
        inverse * (scaled - centre - normal * slope),
        jnp.sum(upstream * normal, axis=0),
        jnp.sum(upstream, axis=0),
    )


def rotate(value, cosine, sine):
    half = ROT // 2
    head = value[..., :ROT]
    turned = jnp.concatenate([-head[..., half:], head[..., :half]], axis=-1)
    return jnp.concatenate([head * cosine + turned * sine, value[..., ROT:]], axis=-1)


def unrotate(grad, cosine, sine):
    half = ROT // 2
    head = grad[..., :ROT]
    moved = head * sine
    back = jnp.concatenate([moved[..., half:], -moved[..., :half]], axis=-1)
    return jnp.concatenate([head * cosine + back, grad[..., ROT:]], axis=-1)


def token_tables(seq_device, seq_lengths, seq_offsets, device, rows):
    slots = jnp.arange(rows, dtype=jnp.int32)
    numbers = jnp.arange(seq_device.shape[0], dtype=jnp.int32)
    inside = (
        (seq_device == device)[:, None]
        & (slots[None, :] >= seq_offsets[:, None])
        & (slots[None, :] < (seq_offsets + seq_lengths)[:, None])
    )
    segment = jnp.sum(jnp.where(inside, numbers[:, None] + 1, 0), axis=0) - 1
    position = jnp.sum(jnp.where(inside, slots[None, :] - seq_offsets[:, None], 0), axis=0)
    return (segment, position)


def attention_scores(query, key, allowed):
    scores = jnp.einsum("qhd,khd->hqk", query, key, preferred_element_type=jnp.float32) * HD ** (
        -0.5
    )
    return jnp.where(allowed[None], scores, -1e30)


def per_device(
    tokens,
    cotangent,
    w_qkv,
    b_qkv,
    w_out,
    b_out,
    w_up,
    b_up,
    w_down,
    b_down,
    ln1_gain,
    ln1_bias,
    ln2_gain,
    ln2_bias,
    seq_device,
    seq_lengths,
    seq_offsets,
):
    rows = tokens.shape[0]
    width = tokens.shape[1]
    heads = width // HD
    half = ROT // 2
    gathered = (
        lax.all_gather(w_qkv, "shard", axis=0, tiled=True),
        lax.all_gather(b_qkv, "shard", axis=0, tiled=True),
        lax.all_gather(w_out, "shard", axis=0, tiled=True),
        lax.all_gather(b_out, "shard", axis=0, tiled=True),
        lax.all_gather(w_up, "shard", axis=0, tiled=True),
        lax.all_gather(b_up, "shard", axis=0, tiled=True),
        lax.all_gather(w_down, "shard", axis=0, tiled=True),
        lax.all_gather(b_down, "shard", axis=0, tiled=True),
        lax.all_gather(ln1_gain, "shard", axis=0, tiled=True),
        lax.all_gather(ln1_bias, "shard", axis=0, tiled=True),
        lax.all_gather(ln2_gain, "shard", axis=0, tiled=True),
        lax.all_gather(ln2_bias, "shard", axis=0, tiled=True),
    )
    (
        wq_all,
        bq_all,
        wo_all,
        bo_all,
        wu_all,
        bu_all,
        wd_all,
        bd_all,
        g1_all,
        c1_all,
        g2_all,
        c2_all,
    ) = gathered
    device = lax.axis_index("shard") * lax.axis_size("replica") + lax.axis_index("replica")
    segment, position = token_tables(seq_device, seq_lengths, seq_offsets, device, rows)
    valid = (segment >= 0).astype(jnp.float32)
    slots = jnp.arange(rows, dtype=jnp.int32)
    allowed = (segment[:, None] == segment[None, :]) & (slots[None, :] <= slots[:, None])
    freqs = 10000.0 ** (-(jnp.arange(half, dtype=jnp.float32) * 2.0) / ROT)
    angle = position.astype(jnp.float32)[:, None] * freqs[None, :]
    angle = jnp.concatenate([angle, angle], axis=-1)[:, None, :]
    cosine, sine = (jnp.cos(angle), jnp.sin(angle))
    x = tokens.astype(jnp.float32)
    normed1, normal1, inverse1 = norm_rows(
        x, g1_all.astype(jnp.float32), c1_all.astype(jnp.float32)
    )
    normed2, normal2, inverse2 = norm_rows(
        x, g2_all.astype(jnp.float32), c2_all.astype(jnp.float32)
    )
    xn1 = normed1.astype(jnp.bfloat16)
    xn2 = normed2.astype(jnp.bfloat16)
    qkv = jnp.dot(xn1, wq_all, preferred_element_type=jnp.float32) + bq_all.astype(jnp.float32)
    query = rotate(qkv[:, :width].reshape(rows, heads, HD), cosine, sine).astype(jnp.bfloat16)
    key = rotate(qkv[:, width : 2 * width].reshape(rows, heads, HD), cosine, sine).astype(
        jnp.bfloat16
    )
    value = qkv[:, 2 * width :].reshape(rows, heads, HD).astype(jnp.bfloat16)
    scores = attention_scores(query, key, allowed)
    top = jnp.max(scores, axis=-1, keepdims=True)
    lse = top + jnp.log(jnp.sum(jnp.exp(scores - top), axis=-1, keepdims=True))
    probs = jnp.exp(scores - lse).astype(jnp.bfloat16)
    context = (
        jnp.einsum("hqk,khd->qhd", probs, value, preferred_element_type=jnp.float32)
        .reshape(rows, width)
        .astype(jnp.bfloat16)
    )
    attn = jnp.dot(context, wo_all, preferred_element_type=jnp.float32) + bo_all.astype(jnp.float32)
    hidden = jnp.dot(xn2, wu_all, preferred_element_type=jnp.float32) + bu_all.astype(jnp.float32)
    normal_cdf = 0.5 * (1.0 + lax.erf(hidden * INV_ROOT_TWO))
    act = (hidden * normal_cdf).astype(jnp.bfloat16)
    mlp = jnp.dot(act, wd_all, preferred_element_type=jnp.float32) + bd_all.astype(jnp.float32)
    mixed = (valid[:, None] * (x + attn + mlp)).astype(jnp.bfloat16)
    regathered = (
        lax.all_gather(w_qkv, "shard", axis=0, tiled=True),
        lax.all_gather(b_qkv, "shard", axis=0, tiled=True),
        lax.all_gather(w_out, "shard", axis=0, tiled=True),
        lax.all_gather(b_out, "shard", axis=0, tiled=True),
        lax.all_gather(w_up, "shard", axis=0, tiled=True),
        lax.all_gather(b_up, "shard", axis=0, tiled=True),
        lax.all_gather(w_down, "shard", axis=0, tiled=True),
        lax.all_gather(b_down, "shard", axis=0, tiled=True),
        lax.all_gather(ln1_gain, "shard", axis=0, tiled=True),
        lax.all_gather(ln1_bias, "shard", axis=0, tiled=True),
        lax.all_gather(ln2_gain, "shard", axis=0, tiled=True),
        lax.all_gather(ln2_bias, "shard", axis=0, tiled=True),
    )
    (
        wq_back,
        bq_back,
        wo_back,
        bo_back,
        wu_back,
        bu_back,
        wd_back,
        bd_back,
        g1_back,
        c1_back,
        g2_back,
        c2_back,
    ) = regathered
    upstream = cotangent.astype(jnp.float32) * valid[:, None]
    upstream_low = upstream.astype(jnp.bfloat16)
    grad_bias_end = jnp.sum(upstream, axis=0)
    grad_w_out = jnp.einsum("ti,tj->ij", context, upstream_low, preferred_element_type=jnp.float32)
    grad_w_down = jnp.einsum("tf,tj->fj", act, upstream_low, preferred_element_type=jnp.float32)
    grad_act = jnp.einsum("tj,fj->tf", upstream_low, wd_back, preferred_element_type=jnp.float32)
    gelu_slope = normal_cdf + hidden * jnp.exp(-0.5 * hidden * hidden) * INV_ROOT_TWO_PI
    grad_hidden = (grad_act * gelu_slope).astype(jnp.bfloat16)
    grad_b_up = jnp.sum(grad_hidden.astype(jnp.float32), axis=0)
    grad_w_up = jnp.einsum("ti,tf->if", xn2, grad_hidden, preferred_element_type=jnp.float32)
    grad_xn2 = jnp.einsum("tf,if->ti", grad_hidden, wu_back, preferred_element_type=jnp.float32)
    grad_context = jnp.einsum(
        "tj,ij->ti", upstream_low, wo_back, preferred_element_type=jnp.float32
    )
    grad_context = grad_context.astype(jnp.bfloat16).reshape(rows, heads, HD)
    again_scores = attention_scores(query, key, allowed)
    weights_soft = jnp.exp(again_scores - lse)
    grad_value = jnp.einsum(
        "hqk,qhd->khd",
        weights_soft.astype(jnp.bfloat16),
        grad_context,
        preferred_element_type=jnp.float32,
    )
    grad_probs = jnp.einsum("qhd,khd->hqk", grad_context, value, preferred_element_type=jnp.float32)
    grad_scores = weights_soft * (
        grad_probs - jnp.sum(weights_soft * grad_probs, axis=-1, keepdims=True)
    )
    grad_scores = grad_scores.astype(jnp.bfloat16)
    grad_query = jnp.einsum(
        "hqk,khd->qhd", grad_scores, key, preferred_element_type=jnp.float32
    ) * HD ** (-0.5)
    grad_key = jnp.einsum(
        "hqk,qhd->khd", grad_scores, query, preferred_element_type=jnp.float32
    ) * HD ** (-0.5)
    grad_query = unrotate(grad_query, cosine, sine).reshape(rows, width)
    grad_key = unrotate(grad_key, cosine, sine).reshape(rows, width)
    grad_qkv = jnp.concatenate(
        [grad_query, grad_key, grad_value.reshape(rows, width)], axis=1
    ).astype(jnp.bfloat16)
    grad_b_qkv = jnp.sum(grad_qkv.astype(jnp.float32), axis=0)
    grad_w_qkv = jnp.einsum("ti,tc->ic", xn1, grad_qkv, preferred_element_type=jnp.float32)
    grad_xn1 = jnp.einsum("tc,ic->ti", grad_qkv, wq_back, preferred_element_type=jnp.float32)
    back_one, grad_g1, grad_c1 = norm_back(grad_xn1, normal1, inverse1, g1_back.astype(jnp.float32))
    back_two, grad_g2, grad_c2 = norm_back(grad_xn2, normal2, inverse2, g2_back.astype(jnp.float32))
    grad_tokens = (upstream + back_one + back_two).astype(jnp.bfloat16)
    shares = (
        lax.psum_scatter(
            grad_w_qkv.astype(jnp.bfloat16), "shard", scatter_dimension=0, tiled=True
        ).astype(jnp.float32),
        lax.psum_scatter(
            grad_b_qkv.astype(jnp.bfloat16), "shard", scatter_dimension=0, tiled=True
        ).astype(jnp.float32),
        lax.psum_scatter(
            grad_w_out.astype(jnp.bfloat16), "shard", scatter_dimension=0, tiled=True
        ).astype(jnp.float32),
        lax.psum_scatter(
            grad_bias_end.astype(jnp.bfloat16), "shard", scatter_dimension=0, tiled=True
        ).astype(jnp.float32),
        lax.psum_scatter(
            grad_w_up.astype(jnp.bfloat16), "shard", scatter_dimension=0, tiled=True
        ).astype(jnp.float32),
        lax.psum_scatter(
            grad_b_up.astype(jnp.bfloat16), "shard", scatter_dimension=0, tiled=True
        ).astype(jnp.float32),
        lax.psum_scatter(
            grad_w_down.astype(jnp.bfloat16), "shard", scatter_dimension=0, tiled=True
        ).astype(jnp.float32),
        lax.psum_scatter(
            grad_bias_end.astype(jnp.bfloat16), "shard", scatter_dimension=0, tiled=True
        ).astype(jnp.float32),
        lax.psum_scatter(
            grad_g1.astype(jnp.bfloat16), "shard", scatter_dimension=0, tiled=True
        ).astype(jnp.float32),
        lax.psum_scatter(
            grad_c1.astype(jnp.bfloat16), "shard", scatter_dimension=0, tiled=True
        ).astype(jnp.float32),
        lax.psum_scatter(
            grad_g2.astype(jnp.bfloat16), "shard", scatter_dimension=0, tiled=True
        ).astype(jnp.float32),
        lax.psum_scatter(
            grad_c2.astype(jnp.bfloat16), "shard", scatter_dimension=0, tiled=True
        ).astype(jnp.float32),
    )
    owned = (
        lax.psum(shares[0].astype(jnp.bfloat16), "replica").astype(jnp.float32),
        lax.psum(shares[1].astype(jnp.bfloat16), "replica").astype(jnp.float32),
        lax.psum(shares[2].astype(jnp.bfloat16), "replica").astype(jnp.float32),
        lax.psum(shares[3].astype(jnp.bfloat16), "replica").astype(jnp.float32),
        lax.psum(shares[4].astype(jnp.bfloat16), "replica").astype(jnp.float32),
        lax.psum(shares[5].astype(jnp.bfloat16), "replica").astype(jnp.float32),
        lax.psum(shares[6].astype(jnp.bfloat16), "replica").astype(jnp.float32),
        lax.psum(shares[7].astype(jnp.bfloat16), "replica").astype(jnp.float32),
        lax.psum(shares[8].astype(jnp.bfloat16), "replica").astype(jnp.float32),
        lax.psum(shares[9].astype(jnp.bfloat16), "replica").astype(jnp.float32),
        lax.psum(shares[10].astype(jnp.bfloat16), "replica").astype(jnp.float32),
        lax.psum(shares[11].astype(jnp.bfloat16), "replica").astype(jnp.float32),
    )
    return (
        mixed,
        grad_tokens,
        owned[0],
        owned[1],
        owned[2],
        owned[3],
        owned[4],
        owned[5],
        owned[6],
        owned[7],
        owned[8],
        owned[9],
        owned[10],
        owned[11],
    )


def solution(mesh):
    return jax.shard_map(
        per_device,
        mesh=mesh,
        in_specs=(
            P(("shard", "replica"), None),
            P(("shard", "replica"), None),
            P("shard", None),
            P("shard"),
            P("shard", None),
            P("shard"),
            P("shard", None),
            P("shard"),
            P("shard", None),
            P("shard"),
            P("shard"),
            P("shard"),
            P("shard"),
            P("shard"),
            P(),
            P(),
            P(),
        ),
        out_specs=(
            P(("shard", "replica"), None),
            P(("shard", "replica"), None),
            P("shard", None),
            P("shard"),
            P("shard", None),
            P("shard"),
            P("shard", None),
            P("shard"),
            P("shard", None),
            P("shard"),
            P("shard"),
            P("shard"),
            P("shard"),
            P("shard"),
        ),
        check_vma=False,
    )
```

profile of v0, /device:TPU:1, one launch (start us, length us, event | category | flops | bytes accessed | tf_op | source)
XLA Modules:
  0.0 590.6 jit_solution(4933671270017732755)
XLA Ops:
  10.0 1.3 fusion.75
  18.4 124.8 %all-reduce.16 = (bf16[3072]{0:T(1024)(128)(2,1)}, bf16[768]{0:T(1024)(128)(2,1)}, bf16[768]{0:T(1024)(128)(2,1)}, bf16[2304]{0:T(1024)(128)(2,1)S(1)}, bf16[768...) all-reduce(bf16[3072]{0:T(1024)(128)(2,1)S(1)} %dynamic-update-slic, ...), channel_id=1, replica_groups=mesh['shard'=32,'replica'=4] {'shard'}, use_global_device_ids=true, to_apply=%add.6 | all-reduce | flops 8448 | bytes 33792
  145.6 1.2 convert_reduce_fusion
  146.8 1.2 fusion.38
  148.8 1.9 convolution_convert_fusion.5
  151.7 3.2 convolution_add_fusion
  158.2 1.8 fusion.5
  166.3 3.1 convolution_convert_fusion.2
  170.1 1.3 convert_element_type.199
  171.4 6.1 %multiply_convert_fusion.1 = (bf16[256,3072]{1,0:T(8,128)(2,1)}, f32[256,3072]{1,0:T(8,128)}) fusion(f32[3072]{0:T(1024)} %convert_element_type.199, bf16[768,3072]{1,0:T(8,128)(2,1)} %all-gather.9.cloned.1.call-done, bf16[256,768]{1,0:T(8,128)(2,1)S(1)} %copy-done, f32[768]{0:T(1024)S(1)} %convert_element_type.197, f32[768]{0:T(1024)S(1)} %convert_element_type.196, ...), kind=kOutput, calls=%fused_computation.14 | convolution fusion | flops 1213857792 | bytes 9850880 | tf_op jit(solution)/shard_map/dot_general | solution.py:155
  177.6 23.2 %all-gather.11.cloned.1.call-done = bf16[3072,768]{1,0:T(8,128)(2,1)} async-done(((bf16[96,768]{1,0:T(8,128)(2,1)}), bf16[3072,768]{1,0:T(8,128)(2,1)}) %all-gather.11.cloned.1.call-update) | async-done | bytes 4718608 | tf_op jit(solution)/shard_map/all_gather | solution.py:100
  200.8 5.9 fusion.76
  207.8 3.8 convolution_convert_fusion.1
  211.7 5.1 convolution_convert_fusion
  219.4 1.4 dynamic-update-slice.3
  221.6 2.3 fusion.66
  223.9 1.9 convolution_convert_fusion.6
  226.6 1.6 convolution_convert_fusion.3
  228.3 4.0 fusion.77
  232.4 1.6 fusion.36
  234.1 1.3 fusion.32
  235.4 121.7 %all-reduce.15 = (bf16[768]{0:T(1024)(128)(2,1)S(1)}, bf16[768]{0:T(1024)(128)(2,1)S(1)}, bf16[2304]{0:T(1024)(128)(2,1)}, bf16[768]{0:T(1024)(128)(2,1)}, bf16[...) all-reduce(bf16[768]{0:T(1024)(128)(2,1)S(1)} %copy-done.36, ...), channel_id=1, replica_groups=mesh['shard'=32,'replica'=4] {'shard'}, use_global_device_ids=true, to_apply=%add.7 | all-reduce | flops 10752 | bytes 43008
  357.1 11.4 %reduce-scatter.9.cloned.1.call-done = bf16[24,3072]{1,0:T(8,128)(2,1)} async-done(((bf16[768,3072]{1,0:T(8,128)(2,1)}), bf16[24,3072]{1,0:T(8,128)(2,1)}) %reduce-scatter.9.cloned.1.call-update) | async-done | bytes 147472 | tf_op jit(solution)/shard_map/reduce_scatter | solution.py:246
  368.5 87.1 %reduce-scatter.11.cloned.1.call-done = bf16[96,768]{1,0:T(8,128)(2,1)} async-done(((bf16[3072,768]{1,0:T(8,128)(2,1)}), bf16[96,768]{1,0:T(8,128)(2,1)}) %reduce-scatter.11.cloned.1.call-update) | async-done | bytes 147472 | tf_op jit(solution)/shard_map/reduce_scatter | solution.py:252
  455.6 4.7 convolution_add_fusion.3
  464.9 69.5 %reduce-scatter.7.cloned.1.call-done = bf16[24,768]{1,0:T(8,128)(2,1)} async-done(((bf16[768,768]{1,0:T(8,128)(2,1)}), bf16[24,768]{1,0:T(8,128)(2,1)}) %reduce-scatter.7.cloned.1.call-update) | async-done | bytes 36880 | tf_op jit(solution)/shard_map/reduce_scatter | solution.py:240
  534.4 14.3 %all-reduce.17 = (bf16[72]{0:T(256)(128)(2,1)S(1)}, bf16[24,768]{1,0:T(8,128)(2,1)S(1)}, bf16[24]{0:T(256)(128)(2,1)S(1)}, bf16[96]{0:T(256)(128)(2,1)S(1)}, bf1...) all-reduce(bf16[72]{0:T(256)(128)(2,1)S(1)} %dynamic-slice.9, ...), channel_id=1, replica_groups=mesh['shard'=32,'replica'=4] {'replica'}, use_global_device_ids=true, to_apply=%region_15.16 | all-reduce | flops 18720 | bytes 74880 | tf_op jit(solution)/shard_map/psum | solution.py:273
  552.5 2.4 fusion.12
  554.9 23.8 %all-reduce.21.cloned.1.call-done = (bf16[24,2304]{1,0:T(8,128)(2,1)}, bf16[24,3072]{1,0:T(8,128)(2,1)}, bf16[96,768]{1,0:T(8,128)(2,1)}) async-done(((bf16[24,2304]{1,0:T(8,128)(2,1)}, bf16[24,3072]{1,0:T(8,128)(2,1)}, bf16[96,768]{1,0:T(8,128)(2,1)}), (bf16[24,2304]{1,0:T(8,128)(2,1)}, bf16[24,3072]{1,0:T(8,128)(2,1)}, bf16[96,768]{1,0:T(8,128)(2,1)})) %all-reduce.21.cloned.1.call-update) | async-done | bytes 405520 | tf_op jit(solution)/shard_map/psum | solution.py:272
  578.7 1.6 convert_element_type.217
  580.3 1.6 convert_element_type.220
  582.0 1.6 convert_element_type.210
  (192 shorter events, 34.3 us)
Async XLA Ops:
  7.2 144.5 %copy-start = (bf16[256,768]{1,0:T(8,128)(2,1)S(1)}, bf16[256,768]{1,0:T(8,128)(2,1)}, u32[]{:S(2)}) copy-start(bf16[256,768]{1,0:T(8,128)(2,1)} %param.17) | copy-start | bytes 1179652
  7.2 141.7 %all-gather.7.cloned.1.call-start = ((), (), s32[]{:S(2)}) async-start(), calls=%async_computation.5 | async-start | bytes 1216512 | tf_op jit(solution)/shard_map/all_gather | solution.py:96
  7.9 143.8 %all-gather.5.cloned.1.call-start = ((), (), s32[]{:S(2)}) async-start(), calls=%async_computation.4 | async-start | bytes 3649536 | tf_op jit(solution)/shard_map/all_gather | solution.py:94
  8.7 162.8 %all-gather.9.cloned.1.call-start = ((), (), s32[]{:S(2)}) async-start(), calls=%async_computation.6 | async-start | bytes 4866048 | tf_op jit(solution)/shard_map/all_gather | solution.py:98
  9.4 191.4 %all-gather.11.cloned.1.call-start = ((), (), s32[]{:S(2)}) async-start(), calls=%async_computation.7 | async-start | bytes 4866048 | tf_op jit(solution)/shard_map/all_gather | solution.py:100
  10.0 347.1 %reduce-scatter.5.cloned.1.call-start = ((), (), s32[]{:S(2)}) async-start(), calls=%async_computation.8 | async-start | bytes 3649536 | tf_op jit(solution)/shard_map/reduce_scatter | solution.py:234
  143.1 11.8 %copy-start.28 = (f32[768]{0:T(1024)}, f32[768]{0:T(1024)S(1)}, u32[]{:S(2)}) copy-start(f32[768]{0:T(1024)S(1)} %convert_element_type.185) | copy-start | bytes 9220
  143.1 11.8 %copy-start.38 = (f32[768]{0:T(1024)}, f32[768]{0:T(1024)S(1)}, u32[]{:S(2)}) copy-start(f32[768]{0:T(1024)S(1)} %convert_element_type.186) | copy-start | bytes 9220
  145.6 12.5 %copy-start.21 = (f32[256,16]{0,1:T(8,128)}, f32[256,16]{0,1:T(8,128)S(1)}, u32[]{:S(2)}) copy-start(f32[256,16]{0,1:T(8,128)S(1)} %get-tuple-element.73) | copy-start | bytes 49156
  146.8 8.1 %copy-start.25 = (f32[256]{0:T(256)}, f32[256]{0:T(256)S(1)}, u32[]{:S(2)}) copy-start(f32[256]{0:T(256)S(1)} %broadcast_multiply_fusion.5) | copy-start | bytes 3076
  148.1 6.9 %copy-start.23 = (f32[256]{0:T(256)}, f32[256]{0:T(256)S(1)}, u32[]{:S(2)}) copy-start(f32[256]{0:T(256)S(1)} %compare_convert_fusion) | copy-start | bytes 3076
  148.1 6.8 %copy-start.31 = (f32[256]{0:T(256)}, f32[256]{0:T(256)S(1)}, u32[]{:S(2)}) copy-start(f32[256]{0:T(256)S(1)} %add_rsqrt_fusion) | copy-start | bytes 3076
  160.7 4.0 copy-start.20
  169.5 199.0 %reduce-scatter.9.cloned.1.call-start = ((), (), s32[]{:S(2)}) async-start(), calls=%async_computation.10 | async-start | bytes 4866048 | tf_op jit(solution)/shard_map/reduce_scatter | solution.py:246
  171.4 29.3 %copy-start.24 = (f32[256]{0:T(256)S(1)}, f32[256]{0:T(256)}, u32[]{:S(2)}) copy-start(f32[256]{0:T(256)} %copy-done.23) | copy-start | bytes 3076
  200.8 7.0 %copy-start.33 = (f32[256]{0:T(256)S(1)}, f32[256]{0:T(256)}, u32[]{:S(2)}) copy-start(f32[256]{0:T(256)} %copy-done.31) | copy-start | bytes 3076
  211.7 243.9 %reduce-scatter.11.cloned.1.call-start = ((), (), s32[]{:S(2)}) async-start(), calls=%async_computation.11 | async-start | bytes 4866048 | tf_op jit(solution)/shard_map/reduce_scatter | solution.py:252
  216.8 317.6 %reduce-scatter.7.cloned.1.call-start = ((), (), s32[]{:S(2)}) async-start(), calls=%async_computation.9 | async-start | bytes 1216512 | tf_op jit(solution)/shard_map/reduce_scatter | solution.py:240
  221.6 6.5 %copy-start.35 = (bf16[768]{0:T(1024)(128)(2,1)}, bf16[768]{0:T(1024)(128)(2,1)S(1)}, u32[]{:S(2)}) copy-start(bf16[768]{0:T(1024)(128)(2,1)S(1)} %dynamic-update-slice.7) | copy-start | bytes 4612
  221.6 4.9 copy-start.1
  228.2 4.1 copy-start.7
  228.2 4.1 copy-start.9
  228.2 4.1 copy-start.19
  228.2 4.1 copy-start.30
  228.2 4.1 copy-start.34
  228.2 350.5 %all-reduce.21.cloned.1.call-start = ((), (), s32[]{:S(2)}) async-start(), calls=%async_computation.12 | async-start | bytes 811008 | tf_op jit(solution)/shard_map/psum | solution.py:272
  228.3 4.1 copy-start.42
  232.4 3.0 copy-start.27
  234.0 221.6 %copy-start.3 = (bf16[256,3072]{1,0:T(8,128)(2,1)S(1)}, bf16[256,3072]{1,0:T(8,128)(2,1)}, u32[]{:S(2)}) copy-start(bf16[256,3072]{1,0:T(8,128)(2,1)} %get-tuple-element.76) | copy-start | bytes 4718596
  455.6 96.9 %copy-start.11 = (bf16[12,64,256]{2,1,0:T(8,128)(2,1)S(1)}, bf16[12,64,256]{2,1,0:T(8,128)(2,1)}, u32[]{:S(2)}) copy-start(bf16[12,64,256]{2,1,0:T(8,128)(2,1)} %copy-done.10) | copy-start | bytes 1179652
  455.6 96.9 %copy-start.16 = (bf16[768,768]{1,0:T(8,128)(2,1)S(1)}, bf16[768,768]{1,0:T(8,128)(2,1)}, u32[]{:S(2)}) copy-start(bf16[768,768]{1,0:T(8,128)(2,1)} %all-gather.7.cloned.1.call-done) | copy-start | bytes 3538948
  549.4 34.7 %copy-start.44 = (f32[24]{0:T(128)}, f32[24]{0:T(128)S(1)}, u32[]{:S(2)}) copy-start(f32[24]{0:T(128)S(1)} %convert_element_type.215) | copy-start | bytes 292
  (22 other events, 36.0 us)
Sparse Core Ops, SparseCore 0:
  10.3 46.4 all-gather.6
  59.2 44.9 all-gather.4
  106.4 46.0 all-gather.8
  154.6 46.1 all-gather.10
  204.4 77.8 reduce-scatter.4
  285.9 82.5 reduce-scatter.8
  372.7 82.8 reduce-scatter.10
  459.1 75.2 reduce-scatter.6
  537.0 41.6 all-reduce.20
where the time goes:
time: 593 us; the launch traced here: 591 us
  blocking collectives  261 us (44%)
  waiting for transfers between devices  218 us (37%)
  matrix products  50.1 us (8%)
  local copies, waits for them, and re-layouts  22.1 us (4%)
  other arithmetic  20.9 us (4%)
  between operations  18.5 us (3%)
    unnamed x2, blocking collectives  246 us
    reduce_scatter x1, waiting for transfers between devices, per_device(): lax.psum_scatter(grad_w_down.astype(jnp.bfloat16), 'shard', scatter_dimen...  87.1 us
    reduce_scatter x1, waiting for transfers between devices, per_device(): lax.psum_scatter(grad_w_out.astype(jnp.bfloat16), 'shard', scatter_dimens...  69.5 us
    psum x1, waiting for transfers between devices, per_device(): lax.psum(shares[0].astype(jnp.bfloat16), 'replica').astype(jnp.float32)  23.8 us
    all_gather x1, waiting for transfers between devices, per_device(): lax.all_gather(w_down, 'shard', axis=0, tiled=True)  23.2 us
    unnamed x115, local copies, waits for them, and re-layouts  18.1 us
    psum x1, blocking collectives, per_device(): lax.psum(shares[1].astype(jnp.bfloat16), 'replica').astype(jnp.float32)  14.3 us
  transfers between devices with their start and end apart: 9, of which 5 were waited for; matrix products, arithmetic and copies ran while one was open for 14% of the time, Pallas kernels for 0%

commit v1 on v0

v1 whole, which is shorter than its diff:
```python
import jax
import jax.numpy as jnp
from jax import lax
from jax.experimental import pallas as pl
from jax.experimental.pallas import tpu as pltpu
from jax.sharding import PartitionSpec as P

HD = 64
ROT = 16


EPS = 1e-05
INV_ROOT_TWO = 0.7071067811865476
INV_ROOT_TWO_PI = 0.3989422804014327


def norm_rows(x, gain, bias):
    mean = jnp.mean(x, axis=-1, keepdims=True)
    centered = x - mean
    var = jnp.mean(centered * centered, axis=-1, keepdims=True)
    inverse = lax.rsqrt(var + EPS)
    normal = centered * inverse
    return (normal * gain + bias, normal, inverse)


def norm_back(upstream, normal, inverse, gain):
    scaled = upstream * gain
    centre = jnp.mean(scaled, axis=-1, keepdims=True)
    slope = jnp.mean(scaled * normal, axis=-1, keepdims=True)
    return (
        inverse * (scaled - centre - normal * slope),
        jnp.sum(upstream * normal, axis=0),
        jnp.sum(upstream, axis=0),
    )


def rotate(value, cosine, sine):
    half = ROT // 2
    head = value[..., :ROT]
    turned = jnp.concatenate([-head[..., half:], head[..., :half]], axis=-1)
    return jnp.concatenate([head * cosine + turned * sine, value[..., ROT:]], axis=-1)


def unrotate(grad, cosine, sine):
    half = ROT // 2
    head = grad[..., :ROT]
    moved = head * sine
    back = jnp.concatenate([moved[..., half:], -moved[..., :half]], axis=-1)
    return jnp.concatenate([head * cosine + back, grad[..., ROT:]], axis=-1)


def token_tables(seq_device, seq_lengths, seq_offsets, device, rows):
    slots = jnp.arange(rows, dtype=jnp.int32)
    numbers = jnp.arange(seq_device.shape[0], dtype=jnp.int32)
    inside = (
        (seq_device == device)[:, None]
        & (slots[None, :] >= seq_offsets[:, None])
        & (slots[None, :] < (seq_offsets + seq_lengths)[:, None])
    )
    segment = jnp.sum(jnp.where(inside, numbers[:, None] + 1, 0), axis=0) - 1
    position = jnp.sum(jnp.where(inside, slots[None, :] - seq_offsets[:, None], 0), axis=0)
    return (segment, position)


def attention_scores(query, key, allowed):
    scores = jnp.einsum("qhd,khd->hqk", query, key, preferred_element_type=jnp.float32) * HD ** (
        -0.5
    )
    return jnp.where(allowed[None], scores, -1e30)


MESH = pl.DeviceIdType.MESH

UNIT = (48, 48, 48, 192, 16)
WIDTH = (2304, 768, 3072, 768, 768)
CUT = (640, 256, 768, 128, 256)
PARTS = 5


def place():
    index = lax.axis_index("shard")
    core = lax.rem(index, 2)
    chip = index // 2
    x = lax.rem(chip, 4)
    y = chip // 4
    first = x * (1 - core) + y * core
    second = y * (1 - core) + x * core
    return core, first, second, 1 + 3 * core, 4 - 3 * core


def around(value, shift):
    return lax.rem(value + shift + 4, 4)


def remote(source, target, sent, received, device):
    return pltpu.make_async_remote_copy(
        src_ref=source, dst_ref=target, send_sem=sent, recv_sem=received, device_id=device, device_id_type=MESH
    )


def gather_kernel(*refs):
    own = refs[:PARTS]
    full = refs[PARTS : 2 * PARTS]
    pair = refs[2 * PARTS : 3 * PARTS]
    unit = refs[3 * PARTS : 4 * PARTS]
    pair_send, pair_recv, send, recv, near_send, near_recv, keep = refs[4 * PARTS :]
    core, first, second, stride_a, stride_b = place()

    def chip(da, db):
        return around(first, da) * stride_a + around(second, db) * stride_b

    def device(da, db):
        return {"shard": chip(da, db) * 2 + core}

    sibling = {"shard": chip(0, 0) * 2 + 1 - core}

    def block(i, da, db, low=0, high=None):
        u, half = UNIT[i], WIDTH[i] // 2
        high = half if high is None else high
        return full[i].at[
            pl.ds(pl.multiple_of(chip(da, db) * u, 16), u),
            pl.ds(pl.multiple_of(core * half + low, 128), high - low),
        ]

    barrier = pltpu.get_barrier_semaphore()
    for target in (device(1, 0), device(-1, 0), device(0, 1), device(0, -1), sibling):
        pl.semaphore_signal(barrier, inc=1, device_id=target, device_id_type=MESH)
    pl.semaphore_wait(barrier, 5)

    started = []
    pairs = []
    for i in range(PARTS):
        half = WIDTH[i] // 2
        copy = remote(
            own[i].at[:, pl.ds(pl.multiple_of((1 - core) * half, 128), half)],
            pair[i],
            pair_send.at[i],
            pair_recv.at[i],
            sibling,
        )
        copy.start()
        pairs.append(copy)

    def push(i, slot, source, target, device_id, arrival):
        copy = remote(source, target, send.at[i, slot], recv.at[i, arrival], device_id)
        copy.start()
        started.append(copy)

    def arrived(i, slot, ref):
        remote(ref, ref, send.at[i, 0], recv.at[i, slot], sibling).wait_recv()

    def hand_over(i, da, db, source=None):
        target = block(i, da, db)
        remote(target if source is None else source, target, near_send.at[i], near_recv.at[i], sibling).start()

    keeps = []
    for i in range(PARTS):
        half = WIDTH[i] // 2
        pairs[i].wait_recv()
        mine = jnp.where(core == 0, own[i][:, :half], own[i][:, half:])
        other = pair[i][...]
        if i == 4:
            unit[i][...] = (mine + other).astype(jnp.bfloat16)
        else:
            rows = jnp.concatenate([jnp.where(core == 0, mine, other), jnp.where(core == 0, other, mine)], axis=0)
            unit[i][...] = rows.astype(jnp.bfloat16)
        here = block(i, 0, 0)
        push(i, 0, unit[i], here, device(1, 0), 0)
        push(i, 1, unit[i], here, device(-1, 0), 1)
        push(i, 2, unit[i], here, device(0, 1), 4)
        push(i, 3, unit[i], here, device(0, -1), 8)
        hand_over(i, 0, 0, unit[i])
        copy = pltpu.make_async_copy(unit[i], here, keep.at[i])
        copy.start()
        keeps.append(copy)
    for i in range(PARTS):
        half, cut = WIDTH[i] // 2, CUT[i]
        arrived(i, 0, block(i, -1, 0))
        push(i, 4, block(i, -1, 0, 0, cut), block(i, -1, 0, 0, cut), device(1, 0), 2)
        push(i, 5, block(i, -1, 0), block(i, -1, 0), device(0, 1), 5)
        push(i, 6, block(i, -1, 0), block(i, -1, 0), device(0, -1), 9)
        hand_over(i, -1, 0)
        arrived(i, 1, block(i, 1, 0))
        push(i, 7, block(i, 1, 0, cut, half), block(i, 1, 0, cut, half), device(-1, 0), 3)
        push(i, 8, block(i, 1, 0), block(i, 1, 0), device(0, 1), 6)
        push(i, 9, block(i, 1, 0), block(i, 1, 0), device(0, -1), 10)
        hand_over(i, 1, 0)
    for i in range(PARTS):
        half, cut = WIDTH[i] // 2, CUT[i]
        arrived(i, 4, block(i, 0, -1))
        push(i, 12, block(i, 0, -1), block(i, 0, -1), device(0, 1), 12)
        hand_over(i, 0, -1)
        arrived(i, 8, block(i, 0, 1))
        hand_over(i, 0, 1)
        arrived(i, 2, block(i, 2, 0, 0, cut))
        arrived(i, 3, block(i, 2, 0, cut, half))
        push(i, 10, block(i, 2, 0), block(i, 2, 0), device(0, 1), 7)
        push(i, 11, block(i, 2, 0), block(i, 2, 0), device(0, -1), 11)
        hand_over(i, 2, 0)
    for i in range(PARTS):
        arrived(i, 5, block(i, -1, -1))
        push(i, 13, block(i, -1, -1), block(i, -1, -1), device(0, 1), 13)
        hand_over(i, -1, -1)
        arrived(i, 9, block(i, -1, 1))
        hand_over(i, -1, 1)
        arrived(i, 10, block(i, 1, 1))
        push(i, 14, block(i, 1, 1), block(i, 1, 1), device(0, -1), 14)
        hand_over(i, 1, 1)
        arrived(i, 6, block(i, 1, -1))
        hand_over(i, 1, -1)
    for i in range(PARTS):
        arrived(i, 11, block(i, 2, 1))
        push(i, 15, block(i, 2, 1), block(i, 2, 1), device(0, -1), 15)
        hand_over(i, 2, 1)
        arrived(i, 7, block(i, 2, -1))
        hand_over(i, 2, -1)
        arrived(i, 12, block(i, 0, 2))
        hand_over(i, 0, 2)
    for i in range(PARTS):
        for slot, da in ((13, -1), (14, 1), (15, 2)):
            arrived(i, slot, block(i, da, 2))
            hand_over(i, da, 2)
    for i in range(PARTS):
        half = WIDTH[i] // 2
        mine = full[i].at[:, pl.ds(pl.multiple_of(core * half, 128), half)]
        other = full[i].at[:, pl.ds(pl.multiple_of((1 - core) * half, 128), half)]
        remote(mine, other, near_send.at[i], near_recv.at[i], sibling).wait()
        keeps[i].wait()
        pairs[i].wait_send()
    for copy in started:
        copy.wait_send()


def gather(w_qkv, w_out, w_up, w_down, small):
    own = [value.astype(jnp.float32) for value in (w_qkv, w_out, w_up, w_down, small)]
    vmem = pl.BlockSpec(memory_space=pltpu.VMEM)
    anywhere = pl.BlockSpec(memory_space=pl.ANY)
    return pl.pallas_call(
        gather_kernel,
        out_shape=[jax.ShapeDtypeStruct((16 * UNIT[i], WIDTH[i]), jnp.bfloat16) for i in range(PARTS)],
        in_specs=[vmem] * PARTS,
        out_specs=[anywhere] * PARTS,
        scratch_shapes=[pltpu.VMEM((own[i].shape[0], WIDTH[i] // 2), jnp.float32) for i in range(PARTS)]
        + [pltpu.VMEM((UNIT[i], WIDTH[i] // 2), jnp.bfloat16) for i in range(PARTS)]
        + [
            pltpu.SemaphoreType.DMA((PARTS,)),
            pltpu.SemaphoreType.DMA((PARTS,)),
            pltpu.SemaphoreType.DMA((PARTS, 16)),
            pltpu.SemaphoreType.DMA((PARTS, 16)),
            pltpu.SemaphoreType.DMA((PARTS,)),
            pltpu.SemaphoreType.DMA((PARTS,)),
            pltpu.SemaphoreType.DMA((PARTS,)),
        ],
        compiler_params=pltpu.CompilerParams(
            collective_id=0, has_side_effects=True, vmem_limit_bytes=24 * 1024 * 1024
        ),
    )(*own)


GRADS = 4
TILES = 36


def scatter_kernel(*refs):
    full = refs[:GRADS]
    small_ref = refs[GRADS]
    outs = refs[GRADS + 1 : 2 * GRADS + 1]
    small_out = refs[2 * GRADS + 1]
    rest = refs[2 * GRADS + 2 :]
    total = rest[:GRADS]
    pair = rest[GRADS : 2 * GRADS]
    far_b = rest[2 * GRADS : 3 * GRADS]
    near_b = rest[3 * GRADS : 4 * GRADS]
    far_a = rest[4 * GRADS : 5 * GRADS]
    near_a = rest[5 * GRADS : 6 * GRADS]
    last = rest[6 * GRADS : 7 * GRADS]
    (
        part, parts_in, whole, small_in, small_sum,
        local, pair_send, pair_recv, send, recv, z_send, z_recv, small_send, small_recv, out_send, out_recv, out_local,
    ) = rest[7 * GRADS :]
    core, first, second, stride_a, stride_b = place()
    depth = lax.axis_index("replica")

    def chip(da, db):
        return around(first, da) * stride_a + around(second, db) * stride_b

    def device(da, db):
        return {"shard": chip(da, db) * 2 + core}

    def deep(dz):
        return {"replica": around(depth, dz)}

    sibling = {"shard": chip(0, 0) * 2 + 1 - core}

    def half_of(i, which):
        half = WIDTH[i] // 2
        return full[i].at[:, pl.ds(pl.multiple_of(which * half, 128), half)]

    def rows(i, where):
        return pl.ds(pl.multiple_of(where * UNIT[i], 16), UNIT[i])

    def in_line(i, a, db):
        return rows(i, a * stride_a + around(second, db) * stride_b)

    barrier = pltpu.get_barrier_semaphore()
    targets = [device(1, 0), device(-1, 0), device(2, 0), device(0, 1), device(0, -1), device(0, 2), sibling]
    targets += [deep(1), deep(2), deep(3)]
    for target in targets:
        pl.semaphore_signal(barrier, inc=1, device_id=target, device_id_type=MESH)
    pl.semaphore_wait(barrier, len(targets))

    started = []

    def start(source, target, sent, received, device_id):
        copy = remote(source, target, sent, received, device_id)
        copy.start()
        started.append(copy)

    def arrived(ref, received):
        remote(ref, ref, send.at[0, 0], received, sibling).wait_recv()

    loads = []
    for i in range(GRADS):
        start(half_of(i, 1 - core), pair[i], pair_send.at[i], pair_recv.at[i], sibling)
        copy = pltpu.make_async_copy(half_of(i, core), total[i], local.at[i])
        copy.start()
        loads.append(copy)
    start(small_ref, small_in.at[0], small_send.at[0], small_recv.at[0], sibling)

    def small_step(step, count, others):
        base = 0 if step == 0 else 3 * step - 2
        for n in range(count):
            arrived(small_in.at[base + n], small_recv.at[base + n])
        value = small_ref[...] if step == 0 else small_sum[step - 1]
        for n in range(count):
            value = value + small_in[base + n]
        small_sum[step] = value
        if others is not None:
            base = 3 * step + 1
            for n, target in enumerate(others):
                start(small_sum.at[step], small_in.at[base + n], small_send.at[base + n], small_recv.at[base + n], target)

    def add_rows(i, where, extra):
        total[i][where, :] = (total[i][where, :].astype(jnp.float32) + extra.astype(jnp.float32)).astype(jnp.bfloat16)

    def add_pair(i, db):
        for a in range(4):
            where = in_line(i, a, db)
            add_rows(i, where, pair[i][where, :])

    for i in range(GRADS):
        loads[i].wait()
        arrived(pair[i], pair_recv.at[i])
        add_pair(i, 2)
        for n, a in enumerate((0, 1)):
            start(total[i].at[in_line(i, a, 2), :], far_b[i].at[n], send.at[i, n], recv.at[i, n], device(0, 1))
        for n, a in enumerate((2, 3)):
            start(total[i].at[in_line(i, a, 2), :], far_b[i].at[2 + n], send.at[i, 2 + n], recv.at[i, 2 + n], device(0, -1))
        add_pair(i, 1)
        for a in (2, 3):
            start(total[i].at[in_line(i, a, 1), :], near_b[i].at[a], send.at[i, 4 + a], recv.at[i, 4 + a], device(0, 1))
        add_pair(i, -1)
        for a in (0, 1):
            start(total[i].at[in_line(i, a, -1), :], near_b[i].at[4 + a], send.at[i, 8 + a], recv.at[i, 8 + a], device(0, -1))
        if i == 0:
            small_step(0, 1, (device(1, 0), device(2, 0), device(-1, 0)))
    for i in range(GRADS):
        for n, a in enumerate((0, 1)):
            arrived(far_b[i].at[n], recv.at[i, n])
            add_rows(i, in_line(i, a, 1), far_b[i][n])
            start(total[i].at[in_line(i, a, 1), :], near_b[i].at[a], send.at[i, 4 + a], recv.at[i, 4 + a], device(0, 1))
        for n, a in enumerate((2, 3)):
            arrived(far_b[i].at[2 + n], recv.at[i, 2 + n])
            add_rows(i, in_line(i, a, -1), far_b[i][2 + n])
            start(total[i].at[in_line(i, a, -1), :], near_b[i].at[4 + a], send.at[i, 8 + a], recv.at[i, 8 + a], device(0, -1))
        add_pair(i, 0)
    small_step(1, 3, (device(0, 1), device(0, 2), device(0, -1)))
    for i in range(GRADS):
        half, cut = WIDTH[i] // 2, CUT[i]
        for n in range(8):
            arrived(near_b[i].at[n], recv.at[i, 4 + n])

        def here(da, db=0):
            return rows(i, chip(da, db))

        for a in range(4):
            where = in_line(i, a, 0)
            value = total[i][where, :].astype(jnp.float32) + near_b[i][a].astype(jnp.float32)
            total[i][where, :] = (value + near_b[i][4 + a].astype(jnp.float32)).astype(jnp.bfloat16)
        start(total[i].at[here(2), pl.ds(0, cut)], far_a[i].at[:, pl.ds(0, cut)], send.at[i, 12], recv.at[i, 12], device(1, 0))
        start(
            total[i].at[here(2), pl.ds(cut, half - cut)],
            far_a[i].at[:, pl.ds(cut, half - cut)],
            send.at[i, 13],
            recv.at[i, 13],
            device(-1, 0),
        )
    small_step(2, 3, (deep(1), deep(2), deep(3)))
    for i in range(GRADS):
        half, cut = WIDTH[i] // 2, CUT[i]
        low, high = pl.ds(0, cut), pl.ds(cut, half - cut)
        one, other = rows(i, chip(1, 0)), rows(i, chip(-1, 0))
        arrived(far_a[i].at[:, low], recv.at[i, 12])
        value = total[i][one, low].astype(jnp.float32) + far_a[i][:, low].astype(jnp.float32)
        total[i][one, low] = value.astype(jnp.bfloat16)
        start(total[i].at[one, :], near_a[i].at[0], send.at[i, 14], recv.at[i, 14], device(1, 0))
        arrived(far_a[i].at[:, high], recv.at[i, 13])
        value = total[i][other, high].astype(jnp.float32) + far_a[i][:, high].astype(jnp.float32)
        total[i][other, high] = value.astype(jnp.bfloat16)
        start(total[i].at[other, :], near_a[i].at[1], send.at[i, 15], recv.at[i, 15], device(-1, 0))

    def tiles():
        n = 0
        for i in range(GRADS):
            for r in range(UNIT[i] // 48):
                for t in range(WIDTH[i] // 256):
                    yield n, i, slice(48 * r, 48 * r + 48), slice(128 * t, 128 * t + 128)
                    n += 1

    for i in range(GRADS):
        arrived(near_a[i].at[0], recv.at[i, 14])
        arrived(near_a[i].at[1], recv.at[i, 15])
        mine = total[i][rows(i, chip(0, 0)), :].astype(jnp.float32)
        last[i][...] = mine + near_a[i][0].astype(jnp.float32) + near_a[i][1].astype(jnp.float32)
    for n, i, r, c in tiles():
        part[n] = last[i][r, c].astype(jnp.bfloat16)
    quarter = TILES // 4

    def share(dz):
        return pl.ds(around(depth, dz) * quarter, quarter)

    for n in range(3):
        start(part.at[share(n + 1)], parts_in.at[n], z_send.at[n], z_recv.at[n], deep(n + 1))
    small_step(3, 3, None)
    small_out[...] = small_sum[3]
    value = part[share(0)].astype(jnp.float32)
    for n in range(3):
        arrived(parts_in.at[n], z_recv.at[n])
        value = value + parts_in[n].astype(jnp.float32)
    whole[share(0)] = value.astype(jnp.bfloat16)
    for n in range(3):
        start(whole.at[share(0)], whole.at[share(0)], z_send.at[3 + n], z_recv.at[3 + n], deep(n + 1))
    for n in range(3):
        arrived(whole.at[share(-n - 1)], z_recv.at[3 + n])
    for n, i, r, c in tiles():
        last[i][r, c] = whole[n].astype(jnp.float32)
    finals = []
    for i in range(GRADS):
        half, own = WIDTH[i] // 2, UNIT[i] // 2
        columns = pl.ds(pl.multiple_of(core * half, 128), half)
        copy = remote(
            last[i].at[pl.ds(pl.multiple_of((1 - core) * own, 8), own), :],
            outs[i].at[:, columns],
            out_send.at[i],
            out_recv.at[i],
            sibling,
        )
        copy.start()
        finals.append(copy)
        copy = pltpu.make_async_copy(
            last[i].at[pl.ds(pl.multiple_of(core * own, 8), own), :], outs[i].at[:, columns], out_local.at[i]
        )
        copy.start()
        finals.append(copy)
    for copy in finals:
        copy.wait()
    for copy in started:
        copy.wait_send()


def scatter(grads, small):
    vmem = pl.BlockSpec(memory_space=pltpu.VMEM)
    anywhere = pl.BlockSpec(memory_space=pl.ANY)
    index = range(GRADS)
    half = [WIDTH[i] // 2 for i in index]
    low = jnp.bfloat16
    dma = pltpu.SemaphoreType.DMA
    return pl.pallas_call(
        scatter_kernel,
        out_shape=[jax.ShapeDtypeStruct((UNIT[i] // 2, WIDTH[i]), jnp.float32) for i in index]
        + [jax.ShapeDtypeStruct(small.shape, jnp.float32)],
        in_specs=[anywhere] * GRADS + [vmem],
        out_specs=[anywhere] * GRADS + [vmem],
        scratch_shapes=[pltpu.VMEM((16 * UNIT[i], half[i]), low) for i in index]
        + [pltpu.VMEM((16 * UNIT[i], half[i]), low) for i in index]
        + [pltpu.VMEM((4, UNIT[i], half[i]), low) for i in index]
        + [pltpu.VMEM((8, UNIT[i], half[i]), low) for i in index]
        + [pltpu.VMEM((UNIT[i], half[i]), low) for i in index]
        + [pltpu.VMEM((2, UNIT[i], half[i]), low) for i in index]
        + [pltpu.VMEM((UNIT[i], half[i]), jnp.float32) for i in index]
        + [
            pltpu.VMEM((TILES, 48, 128), low),
            pltpu.VMEM((3, TILES // 4, 48, 128), low),
            pltpu.VMEM((TILES, 48, 128), low),
            pltpu.VMEM((10, 16, 768), jnp.float32),
            pltpu.VMEM((4, 16, 768), jnp.float32),
            dma((GRADS,)),
            dma((GRADS,)),
            dma((GRADS,)),
            dma((GRADS, 16)),
            dma((GRADS, 16)),
            dma((6,)),
            dma((6,)),
            dma((10,)),
            dma((10,)),
            dma((GRADS,)),
            dma((GRADS,)),
            dma((GRADS,)),
        ],
        compiler_params=pltpu.CompilerParams(
            collective_id=1, has_side_effects=True, vmem_limit_bytes=48 * 1024 * 1024
        ),
    )(*grads, small)


def per_device(
    tokens,
    cotangent,
    w_qkv,
    b_qkv,
    w_out,
    b_out,
    w_up,
    b_up,
    w_down,
    b_down,
    ln1_gain,
    ln1_bias,
    ln2_gain,
    ln2_bias,
    seq_device,
    seq_lengths,
    seq_offsets,
):
    rows = tokens.shape[0]
    width = tokens.shape[1]
    heads = width // HD
    half = ROT // 2
    values = (b_qkv, b_up, b_out, b_down, ln1_gain, ln1_bias, ln2_gain, ln2_bias)
    index = lax.axis_index("shard")
    small = jnp.concatenate(
        [
            lax.dynamic_update_slice(
                jnp.zeros((value.shape[0] * 32,), jnp.float32), value.astype(jnp.float32), (index * value.shape[0],)
            )
            for value in values
        ]
        + [jnp.zeros((3 * width,), jnp.float32)]
    ).reshape(16, width)
    wq_all, wo_all, wu_all, wd_all, small_all = gather(w_qkv, w_out, w_up, w_down, small)
    small_all = jnp.sum(small_all.astype(jnp.float32).reshape(16, 16, width), axis=0)
    bq_all = small_all[0:3].reshape(3 * width)
    bu_all = small_all[3:7].reshape(4 * width)
    bo_all, bd_all, g1_all, c1_all, g2_all, c2_all = (small_all[row] for row in range(7, 13))
    device = lax.axis_index("shard") * lax.axis_size("replica") + lax.axis_index("replica")
    segment, position = token_tables(seq_device, seq_lengths, seq_offsets, device, rows)
    valid = (segment >= 0).astype(jnp.float32)
    slots = jnp.arange(rows, dtype=jnp.int32)
    allowed = (segment[:, None] == segment[None, :]) & (slots[None, :] <= slots[:, None])
    freqs = 10000.0 ** (-(jnp.arange(half, dtype=jnp.float32) * 2.0) / ROT)
    angle = position.astype(jnp.float32)[:, None] * freqs[None, :]
    angle = jnp.concatenate([angle, angle], axis=-1)[:, None, :]
    cosine, sine = (jnp.cos(angle), jnp.sin(angle))
    x = tokens.astype(jnp.float32)
    normed1, normal1, inverse1 = norm_rows(
        x, g1_all.astype(jnp.float32), c1_all.astype(jnp.float32)
    )
    normed2, normal2, inverse2 = norm_rows(
        x, g2_all.astype(jnp.float32), c2_all.astype(jnp.float32)
    )
    xn1 = normed1.astype(jnp.bfloat16)
    xn2 = normed2.astype(jnp.bfloat16)
    qkv = jnp.dot(xn1, wq_all, preferred_element_type=jnp.float32) + bq_all.astype(jnp.float32)
    query = rotate(qkv[:, :width].reshape(rows, heads, HD), cosine, sine).astype(jnp.bfloat16)
    key = rotate(qkv[:, width : 2 * width].reshape(rows, heads, HD), cosine, sine).astype(
        jnp.bfloat16
    )
    value = qkv[:, 2 * width :].reshape(rows, heads, HD).astype(jnp.bfloat16)
    scores = attention_scores(query, key, allowed)
    top = jnp.max(scores, axis=-1, keepdims=True)
    lse = top + jnp.log(jnp.sum(jnp.exp(scores - top), axis=-1, keepdims=True))
    probs = jnp.exp(scores - lse).astype(jnp.bfloat16)
    context = (
        jnp.einsum("hqk,khd->qhd", probs, value, preferred_element_type=jnp.float32)
        .reshape(rows, width)
        .astype(jnp.bfloat16)
    )
    attn = jnp.dot(context, wo_all, preferred_element_type=jnp.float32) + bo_all.astype(jnp.float32)
    hidden = jnp.dot(xn2, wu_all, preferred_element_type=jnp.float32) + bu_all.astype(jnp.float32)
    normal_cdf = 0.5 * (1.0 + lax.erf(hidden * INV_ROOT_TWO))
    act = (hidden * normal_cdf).astype(jnp.bfloat16)
    mlp = jnp.dot(act, wd_all, preferred_element_type=jnp.float32) + bd_all.astype(jnp.float32)
    mixed = (valid[:, None] * (x + attn + mlp)).astype(jnp.bfloat16)
    upstream = cotangent.astype(jnp.float32) * valid[:, None]
    upstream_low = upstream.astype(jnp.bfloat16)
    grad_bias_end = jnp.sum(upstream, axis=0)
    grad_w_out = jnp.einsum("ti,tj->ij", context, upstream_low, preferred_element_type=jnp.float32)
    grad_w_down = jnp.einsum("tf,tj->fj", act, upstream_low, preferred_element_type=jnp.float32)
    grad_act = jnp.einsum("tj,fj->tf", upstream_low, wd_all, preferred_element_type=jnp.float32)
    gelu_slope = normal_cdf + hidden * jnp.exp(-0.5 * hidden * hidden) * INV_ROOT_TWO_PI
    grad_hidden = (grad_act * gelu_slope).astype(jnp.bfloat16)
    grad_b_up = jnp.sum(grad_hidden.astype(jnp.float32), axis=0)
    grad_w_up = jnp.einsum("ti,tf->if", xn2, grad_hidden, preferred_element_type=jnp.float32)
    grad_xn2 = jnp.einsum("tf,if->ti", grad_hidden, wu_all, preferred_element_type=jnp.float32)
    grad_context = jnp.einsum(
        "tj,ij->ti", upstream_low, wo_all, preferred_element_type=jnp.float32
    )
    grad_context = grad_context.astype(jnp.bfloat16).reshape(rows, heads, HD)
    again_scores = attention_scores(query, key, allowed)
    weights_soft = jnp.exp(again_scores - lse)
    grad_value = jnp.einsum(
        "hqk,qhd->khd",
        weights_soft.astype(jnp.bfloat16),
        grad_context,
        preferred_element_type=jnp.float32,
    )
    grad_probs = jnp.einsum("qhd,khd->hqk", grad_context, value, preferred_element_type=jnp.float32)
    grad_scores = weights_soft * (
        grad_probs - jnp.sum(weights_soft * grad_probs, axis=-1, keepdims=True)
    )
    grad_scores = grad_scores.astype(jnp.bfloat16)
    grad_query = jnp.einsum(
        "hqk,khd->qhd", grad_scores, key, preferred_element_type=jnp.float32
    ) * HD ** (-0.5)
    grad_key = jnp.einsum(
        "hqk,qhd->khd", grad_scores, query, preferred_element_type=jnp.float32
    ) * HD ** (-0.5)
    grad_query = unrotate(grad_query, cosine, sine).reshape(rows, width)
    grad_key = unrotate(grad_key, cosine, sine).reshape(rows, width)
    grad_qkv = jnp.concatenate(
        [grad_query, grad_key, grad_value.reshape(rows, width)], axis=1
    ).astype(jnp.bfloat16)
    grad_b_qkv = jnp.sum(grad_qkv.astype(jnp.float32), axis=0)
    grad_w_qkv = jnp.einsum("ti,tc->ic", xn1, grad_qkv, preferred_element_type=jnp.float32)
    grad_xn1 = jnp.einsum("tc,ic->ti", grad_qkv, wq_all, preferred_element_type=jnp.float32)
    back_one, grad_g1, grad_c1 = norm_back(grad_xn1, normal1, inverse1, g1_all.astype(jnp.float32))
    back_two, grad_g2, grad_c2 = norm_back(grad_xn2, normal2, inverse2, g2_all.astype(jnp.float32))
    grad_tokens = (upstream + back_one + back_two).astype(jnp.bfloat16)
    small_grad = jnp.concatenate(
        [grad_b_qkv, grad_b_up, grad_bias_end, grad_g1, grad_c1, grad_g2, grad_c2, jnp.zeros((4 * width,), jnp.float32)]
    ).reshape(16, width)
    low = jnp.bfloat16
    out_qkv, out_out, out_up, out_down, small_out = scatter(
        [grad_w_qkv.astype(low), grad_w_out.astype(low), grad_w_up.astype(low), grad_w_down.astype(low)], small_grad
    )
    flat = small_out.reshape(16 * width)

    def owned(row, size):
        return lax.dynamic_slice(flat, (row * width + index * size,), (size,))

    end = owned(7, 24)
    return (
        mixed,
        grad_tokens,
        out_qkv,
        owned(0, 72),
        out_out,
        end,
        out_up,
        owned(3, 96),
        out_down,
        end,
        owned(8, 24),
        owned(9, 24),
        owned(10, 24),
        owned(11, 24),
    )


def solution(mesh):
    return jax.shard_map(
        per_device,
        mesh=mesh,
        in_specs=(
            P(("shard", "replica"), None),
            P(("shard", "replica"), None),
            P("shard", None),
            P("shard"),
            P("shard", None),
            P("shard"),
            P("shard", None),
            P("shard"),
            P("shard", None),
            P("shard"),
            P("shard"),
            P("shard"),
            P("shard"),
            P("shard"),
            P(),
            P(),
            P(),
        ),
        out_specs=(
            P(("shard", "replica"), None),
            P(("shard", "replica"), None),
            P("shard", None),
            P("shard"),
            P("shard", None),
            P("shard"),
            P("shard", None),
            P("shard"),
            P("shard", None),
            P("shard"),
            P("shard"),
            P("shard"),
            P("shard"),
            P("shard"),
        ),
        check_vma=False,
    )
```

time: 593 us -> 200 us (0.34)
  blocking collectives: 261 us -> 0 us
  waiting for transfers between devices: 218 us -> 0 us
  Pallas kernels: 0 us -> 116 us
  between operations: 18.5 us -> 1.66 us
  matrix products: 50.1 us -> 39.5 us
    unnamed x2 -> x0, blocking collectives: 246 us -> none
    reduce_scatter x4 -> x0, waiting for transfers between devices: 168 us -> none  [the longest x1 87.1 us: per_device(): lax.psum_scatter(grad_w_down.astype(jnp.bfloat16), 'shard', scatter_dimen...]
    pallas_call x0 -> x2, Pallas kernels: none -> 116 us  [the longest x1 67.5 us: scatter(): pl.pallas_call(scatter_kernel, out_shape=[jax.ShapeDtypeStruct((UNIT[i] /...]
    psum x1 -> x0, waiting for transfers between devices: 23.8 us -> none  [per_device(): lax.psum(shares[0].astype(jnp.bfloat16), 'replica').astype(jnp.float32)]
    all_gather x4 -> x0, waiting for transfers between devices: 23.2 us -> none  [the longest x1 23.2 us: per_device(): lax.all_gather(w_down, 'shard', axis=0, tiled=True)]
    psum x1 -> x0, blocking collectives: 14.3 us -> none  [per_device(): lax.psum(shares[1].astype(jnp.bfloat16), 'replica').astype(jnp.float32)]
    convert_element_type x20 -> x4, other arithmetic: 11.2 us -> 3.56 us  [gather(): value.astype(jnp.float32)]
    dynamic_update_slice x0 -> x8, other arithmetic: none -> 6.18 us  [per_device(): lax.dynamic_update_slice(jnp.zeros((value.shape[0] * 32,), jnp.float32),...]
  transfers between devices with their start and end apart: 9 -> 0, of which waited for: 5 -> 0; matrix products, arithmetic and copies ran while one was open for 14% -> 0% of each run, Pallas kernels for 0% -> 0%
where the time goes in v1:
time: 200 us; the launch traced here: 199 us
  Pallas kernels  116 us (58%)
  matrix products  39.5 us (20%)
  local copies, waits for them, and re-layouts  24.3 us (12%)
  other arithmetic  17.4 us (9%)
    pallas_call x1, Pallas kernels, scatter(): pl.pallas_call(scatter_kernel, out_shape=[jax.ShapeDtypeStruct((UNIT[i] /...  67.5 us
    pallas_call x1, Pallas kernels, gather(): pl.pallas_call(gather_kernel, out_shape=[jax.ShapeDtypeStruct((16 * UNIT[...  48.6 us
    unnamed x124, local copies, waits for them, and re-layouts  16.5 us
    dynamic_update_slice x8, other arithmetic, per_device(): lax.dynamic_update_slice(jnp.zeros((value.shape[0] * 32,), jnp.float32),...  6.18 us
    dot_general x1, matrix products, per_device(): jnp.dot(xn2, wu_all, preferred_element_type=jnp.float32)  5.48 us
    dot_general x1, matrix products, per_device(): jnp.einsum('ti,tf->if', xn2, grad_hidden, preferred_element_type=jnp.floa...  5.21 us
    dot_general x1, matrix products, per_device(): jnp.dot(act, wd_all, preferred_element_type=jnp.float32)  4.24 us

profile of v1, /device:TPU:1, one launch (start us, length us, event | category | flops | bytes accessed | tf_op | source)
XLA Modules:
  0.0 199.0 jit_solution(11470550323953721888)
XLA Ops:
  7.0 0.9 convert_element_type.126.refs_2_
  7.9 0.9 convert_element_type.127.refs_3_
  8.9 0.9 convert_element_type.124.refs_0_
  10.6 48.6 %shard_map.272 = (bf16[768,2304]{1,0:T(8,128)(2,1)S(1)}, bf16[768,768]{1,0:T(8,128)(2,1)S(1)}, bf16[768,3072]{1,0:T(8,128)(2,1)S(1)}, bf16[3072,768]{1,0:T(8,128)(2,1)S(1)}, bf16[256,768]{1,0:T(8,128)(2,1)S(1)}) custom-call(f32[24,2304]{1,0:T(8,128)S(1)} %convert_element_type.124.refs_0_, f32[24,768]{1,0:T(8,128)S(1)} %convert_element_type.125.refs_1_, ...), custom_call_target="tpu_custom_call" | custom-call | tf_op jit(solution)/shard_map/pallas_call | solution.py:238
  59.2 2.1 %copy-done = bf16[3072,768]{1,0:T(8,128)(2,1)} copy-done((bf16[3072,768]{1,0:T(8,128)(2,1)}, bf16[3072,768]{1,0:T(8,128)(2,1)S(1)}, u32[]{:S(2)}) %copy-start) | copy-done | bytes 4718616
  61.3 2.2 %copy-done.1 = bf16[768,3072]{1,0:T(8,128)(2,1)} copy-done((bf16[768,3072]{1,0:T(8,128)(2,1)}, bf16[768,3072]{1,0:T(8,128)(2,1)S(1)}, u32[]{:S(2)}) %copy-start.1) | copy-done | bytes 4718616
  63.5 1.8 copy-done.2
  67.2 3.2 %convolution_add_fusion = f32[256,2304]{1,0:T(8,128)S(1)} fusion(bf16[768,2304]{1,0:T(8,128)(2,1)} %copy-done.2, f32[2304]{0:T(1024)S(1)} %add.200, bf16[256,768]{1,0:T(8,128)(2,1)S(1)} %copy-done.7, f32[768]{0:T(1024)S(1)} %get-tuple-element.50, f32[768]{0:T(1024)S(1)} %get-tuple-element.51, f32[256]{0:T(256)S(1)} %add_rsqrt_fusion, ...), kind=kOutput, calls=%fused_computation.4 | convolution fusion | flops 907739136 | bytes 6308864 | tf_op jit(solution)/shard_map/dot_general | solution.py:573
  70.4 1.4 copy-done.10
  71.9 1.2 copy.56
  73.4 1.0 slice_negate_fusion.2
  74.9 1.0 fusion.48
  75.9 1.1 slice.177
  77.9 1.6 copy-done.4
  80.8 1.2 slice.173
  83.4 1.3 convolution_convert_fusion.5
  84.7 1.2 copy.59
  85.9 3.1 %multiply_reduce_fusion = (f32[12,256]{1,0:T(8,128)S(1)}, f32[12,256,256]{1,2,0:T(8,128)S(1)}) fusion(f32[12,256,256]{1,2,0:T(8,128)} %copy-done.4, f32[12,256]{1,0:T(8,128)} %log_add_fusion, pred[256,256]{0,1:T(8,128)(4,1)S(1)} %fusion.43, bf16[256,12,64]{0,2,1:T(8,128)(2,1)S(1)} %bitcast.51, bf16[256,12,64]{0,2,1:T(8,128)(2,1)S(1)} %bitcast.49), kind=kOutput, calls=%fused_computation.14 | convolution fusion | flops 104592384 | bytes 7168000 | tf_op jit(solution)/shard_map/qhd,khd->hqk/dot_general | solution.py:617
  89.0 0.9 multiply_convert_fusion
  91.3 0.8 convolution_convert_fusion.4
  93.4 5.5 %multiply_convert_fusion.1 = (bf16[256,3072]{1,0:T(8,128)(2,1)}, f32[256,3072]{1,0:T(8,128)S(1)}) fusion(f32[3072]{0:T(1024)S(1)} %add.213, bf16[768,3072]{1,0:T(8,128)(2,1)} %copy-done.1, bf16[256,768]{1,0:T(8,128)(2,1)S(1)} %copy-done.7, f32[768]{0:T(1024)S(1)} %copy-done.30, f32[768]{0:T(1024)S(1)} %copy-done.23, f32[256]{0:T(256)S(1)} %copy-done.39, ...), kind=kOutput, calls=%fused_computation.15 | convolution fusion | flops 1213857792 | bytes 9850880 | tf_op jit(solution)/shard_map/dot_general | solution.py:589
  99.0 3.7 %convert_reduce_fusion = (f32[3072]{0:T(1024)S(1)}, bf16[256,3072]{1,0:T(8,128)(2,1)S(1)}) fusion(f32[256,3072]{1,0:T(8,128)S(1)} %get-tuple-element.80, bf16[3072,768]{1,0:T(8,128)(2,1)S(1)} %bitcast.40, bf16[256,768]{1,0:T(8,128)(2,1)S(1)} %copy-done.8, f32[256]{0:T(256)S(1)} %copy-done.32), kind=kOutput, calls=%fused_computation.12 | convolution fusion | flops 1217983488 | bytes 9843712 | tf_op jit(solution)/shard_map/tj,fj->tf/dot_general | solution.py:599
  102.8 1.4 fusion.75
  104.2 1.0 copy-done.3
  105.5 1.6 fusion.36
  107.1 1.3 fusion.39
  108.5 5.2 %convolution_convert_fusion.1.refs_2_ = bf16[768,3072]{1,0:T(8,128)(2,1)} fusion(bf16[256,3072]{1,0:T(8,128)(2,1)} %copy-done.17, bf16[256,768]{1,0:T(8,128)(2,1)S(1)} %copy-done.7, f32[768]{0:T(1024)S(1)} %copy-done.30, f32[768]{0:T(1024)S(1)} %copy-done.23, f32[256]{0:T(256)S(1)} %copy-done.39, f32[256]{0:T(256)S(1)} %copy-done.34), kind=kOutput, calls=%fused_computation.1 | convolution fusion | flops 1211498496 | bytes 6692864 | tf_op jit(solution)/shard_map/ti,tf->if/dot_general | solution.py:603
  113.7 1.3 convolution_convert_fusion.2.refs_0_
  117.0 3.8 %convolution_convert_fusion.refs_3_ = bf16[3072,768]{1,0:T(8,128)(2,1)} fusion(bf16[256,3072]{1,0:T(8,128)(2,1)S(1)} %copy-done.9, bf16[256,768]{1,0:T(8,128)(2,1)S(1)} %copy-done.8, f32[256]{0:T(256)S(1)} %copy-done.32), kind=kOutput, calls=%fused_computation | convolution fusion | flops 1210908672 | bytes 6685696 | tf_op jit(solution)/shard_map/tf,tj->fj/dot_general | solution.py:598
  120.8 67.5 %shard_map.273 = (f32[24,2304]{1,0:T(8,128)S(1)}, f32[24,768]{1,0:T(8,128)S(1)}, f32[24,3072]{1,0:T(8,128)S(1)}, f32[96,768]{1,0:T(8,128)S(1)}, f32[16,768]{1,0:T(8,128)S(1)}) custom-call(bf16[768,2304]{1,0:T(8,128)(2,1)S(1)} %convolution_convert_fusion.2.refs_0_, bf16[768,768]{1,0:T(8,128)(2,1)S(1)} %convolution_convert_fusion.3.refs_1_, ...), custom_call_target="tpu_custom_call" | custom-call | tf_op jit(solution)/shard_map/pallas_call | solution.py:478
  190.2 4.2 %convolution_add_fusion.3 = f32[256,768]{1,0:T(8,128)S(1)} fusion(bf16[256,3072]{1,0:T(8,128)(2,1)} %get-tuple-element.79, bf16[3072,768]{1,0:T(8,128)(2,1)} %copy-done, f32[768]{0:T(1024)S(1)} %copy-done.42), kind=kOutput, calls=%fused_computation.32 | convolution fusion | flops 1208156160 | bytes 7080960 | tf_op jit(solution)/shard_map/dot_general | solution.py:592
  194.4 1.3 fusion.12
  (192 shorter events, 23.1 us)
Async XLA Ops:
  0.6 65.3 %copy-start.7 = (bf16[256,768]{1,0:T(8,128)(2,1)S(1)}, bf16[256,768]{1,0:T(8,128)(2,1)}, u32[]{:S(2)}) copy-start(bf16[256,768]{1,0:T(8,128)(2,1)} %param.17) | copy-start | bytes 1179652
  59.2 2.1 %copy-start = (bf16[3072,768]{1,0:T(8,128)(2,1)}, bf16[3072,768]{1,0:T(8,128)(2,1)S(1)}, u32[]{:S(2)}) copy-start(bf16[3072,768]{1,0:T(8,128)(2,1)S(1)} %get-tuple-element.28) | copy-start | bytes 14155780
  61.3 2.2 %copy-start.1 = (bf16[768,3072]{1,0:T(8,128)(2,1)}, bf16[768,3072]{1,0:T(8,128)(2,1)S(1)}, u32[]{:S(2)}) copy-start(bf16[768,3072]{1,0:T(8,128)(2,1)S(1)} %get-tuple-element.27) | copy-start | bytes 14155780
  71.8 2.6 %copy-start.46 = (s32[256]{0:T(256)S(1)}, s32[256]{0:T(256)}, u32[]{:S(2)}) copy-start(s32[256]{0:T(256)} %param.31) | copy-start | bytes 3076
  71.8 2.6 %copy-start.41 = (s32[256]{0:T(256)S(1)}, s32[256]{0:T(256)}, u32[]{:S(2)}) copy-start(s32[256]{0:T(256)} %param.33) | copy-start | bytes 3076
  71.8 2.6 %copy-start.45 = (s32[256]{0:T(256)S(1)}, s32[256]{0:T(256)}, u32[]{:S(2)}) copy-start(s32[256]{0:T(256)} %param.32) | copy-start | bytes 3076
  74.7 2.4 %copy-start.40 = (s32[256]{0:T(256)}, s32[256]{0:T(256)S(1)}, u32[]{:S(2)}) copy-start(s32[256]{0:T(256)S(1)} %get-tuple-element.52) | copy-start | bytes 3076
  74.9 2.2 %copy-start.26 = (f32[256,16]{0,1:T(8,128)}, f32[256,16]{0,1:T(8,128)S(1)}, u32[]{:S(2)}) copy-start(f32[256,16]{0,1:T(8,128)S(1)} %get-tuple-element.77) | copy-start | bytes 49156
  74.9 2.2 %copy-start.28 = (f32[256,16]{0,1:T(8,128)}, f32[256,16]{0,1:T(8,128)S(1)}, u32[]{:S(2)}) copy-start(f32[256,16]{0,1:T(8,128)S(1)} %get-tuple-element.78) | copy-start | bytes 49156
  77.9 5.5 %copy-start.8 = (bf16[256,768]{1,0:T(8,128)(2,1)S(1)}, bf16[256,768]{1,0:T(8,128)(2,1)}, u32[]{:S(2)}) copy-start(bf16[256,768]{1,0:T(8,128)(2,1)} %param.18) | copy-start | bytes 1179652
  85.9 3.1 %copy-start.5 = (f32[12,256,256]{1,2,0:T(8,128)S(1)}, f32[12,256,256]{1,2,0:T(8,128)}, u32[]{:S(2)}) copy-start(f32[12,256,256]{1,2,0:T(8,128)} %copy-done.4) | copy-start | bytes 9437188
  85.9 3.1 %copy-start.24 = (f32[12,256]{1,0:T(8,128)S(1)}, f32[12,256]{1,0:T(8,128)}, u32[]{:S(2)}) copy-start(f32[12,256]{1,0:T(8,128)} %log_add_fusion) | copy-start | bytes 36868
  91.2 13.0 %copy-start.11 = (bf16[256,12,64]{0,2,1:T(8,128)(2,1)}, bf16[256,12,64]{0,2,1:T(8,128)(2,1)S(1)}, u32[]{:S(2)}) copy-start(bf16[256,12,64]{0,2,1:T(8,128)(2,1)S(1)} %pad_maximum_fusion.3) | copy-start | bytes 1179652
  91.3 2.1 %copy-start.23 = (f32[768]{0:T(1024)S(1)}, f32[768]{0:T(1024)}, u32[]{:S(2)}) copy-start(f32[768]{0:T(1024)} %get-tuple-element.49) | copy-start | bytes 9220
  91.3 2.1 %copy-start.30 = (f32[768]{0:T(1024)S(1)}, f32[768]{0:T(1024)}, u32[]{:S(2)}) copy-start(f32[768]{0:T(1024)} %get-tuple-element.48) | copy-start | bytes 9220
  92.9 6.0 %slice-start = ((s8[4718592]{0:T(1024)(128)(4,1)}), s8[524288]{0:T(1024)(128)(4,1)S(1)}, s32[]{:S(2)}) async-start(s8[4718592]{0:T(1024)(128)(4,1)} %bitcast.39), calls=%async_computation | async-start | bytes 1048576
  93.4 5.5 %slice-start.1 = ((s8[4718592]{0:T(1024)(128)(4,1)}), s8[4194304]{0:T(1024)(128)(4,1)S(1)}, s32[]{:S(2)}) async-start(s8[4718592]{0:T(1024)(128)(4,1)} %bitcast.39), calls=%async_computation.1 | async-start | bytes 8388608
  93.4 5.5 %copy-start.32 = (f32[256]{0:T(256)S(1)}, f32[256]{0:T(256)}, u32[]{:S(2)}) copy-start(f32[256]{0:T(256)} %copy-done.31) | copy-start | bytes 3076
  93.4 9.3 %slice-start.2 = ((s8[4718592]{0:T(1024)(128)(4,1)}), s8[4194304]{0:T(1024)(128)(4,1)S(1)}, s32[]{:S(2)}) async-start(s8[4718592]{0:T(1024)(128)(4,1)} %bitcast.41), calls=%async_computation.2 | async-start | bytes 8388608
  98.9 3.8 %slice-start.3 = ((s8[4718592]{0:T(1024)(128)(4,1)}), s8[524288]{0:T(1024)(128)(4,1)S(1)}, s32[]{:S(2)}) async-start(s8[4718592]{0:T(1024)(128)(4,1)} %bitcast.41), calls=%async_computation.3 | async-start | bytes 1048576
  102.7 2.5 %copy-start.3 = (bf16[768,2304]{1,0:T(8,128)(2,1)S(1)}, bf16[768,2304]{1,0:T(8,128)(2,1)}, u32[]{:S(2)}) copy-start(bf16[768,2304]{1,0:T(8,128)(2,1)} %copy-done.2) | copy-start | bytes 10616836
  102.7 2.6 %copy-start.14 = (bf16[256,12,64]{0,2,1:T(8,128)(2,1)S(1)}, bf16[256,12,64]{0,2,1:T(8,128)(2,1)}, u32[]{:S(2)}) copy-start(bf16[256,12,64]{0,2,1:T(8,128)(2,1)} %copy-done.13) | copy-start | bytes 1179652
  102.8 2.7 %copy-start.21 = (bf16[12,64,256]{2,1,0:T(8,128)(2,1)S(1)}, bf16[12,64,256]{2,1,0:T(8,128)(2,1)}, u32[]{:S(2)}) copy-start(bf16[12,64,256]{2,1,0:T(8,128)(2,1)} %copy-done.20) | copy-start | bytes 1179652
  102.8 2.7 %copy-start.37 = (f32[768]{0:T(1024)S(1)}, f32[768]{0:T(1024)}, u32[]{:S(2)}) copy-start(f32[768]{0:T(1024)} %copy-done.36) | copy-start | bytes 9220
  108.5 5.2 %copy-start.12 = (bf16[256,12,64]{0,2,1:T(8,128)(2,1)S(1)}, bf16[256,12,64]{0,2,1:T(8,128)(2,1)}, u32[]{:S(2)}) copy-start(bf16[256,12,64]{0,2,1:T(8,128)(2,1)} %copy-done.11) | copy-start | bytes 1179652
  108.5 5.2 %copy-start.22 = (bf16[12,64,256]{2,1,0:T(8,128)(2,1)S(1)}, bf16[12,64,256]{2,1,0:T(8,128)(2,1)}, u32[]{:S(2)}) copy-start(bf16[12,64,256]{2,1,0:T(8,128)(2,1)} %copy-done.20) | copy-start | bytes 1179652
  108.5 5.2 %copy-start.44 = (f32[768]{0:T(1024)S(1)}, f32[768]{0:T(1024)}, u32[]{:S(2)}) copy-start(f32[768]{0:T(1024)} %copy-done.43) | copy-start | bytes 9220
  116.4 4.4 %copy-start.15 = (bf16[12,64,256]{2,1,0:T(8,128)(2,1)}, bf16[12,64,256]{2,1,0:T(8,128)(2,1)S(1)}, u32[]{:S(2)}) copy-start(bf16[12,64,256]{2,1,0:T(8,128)(2,1)S(1)} %convolution_convert_fusion.6) | copy-start | bytes 1179652
  120.8 69.4 %copy-start.42 = (f32[768]{0:T(1024)S(1)}, f32[768]{0:T(1024)}, u32[]{:S(2)}) copy-start(f32[768]{0:T(1024)} %get-tuple-element.47) | copy-start | bytes 9220
  189.0 6.8 %copy-start.47 = (f32[24]{0:T(128)}, f32[24]{0:T(128)S(1)}, u32[]{:S(2)}) copy-start(f32[24]{0:T(128)S(1)} %get-tuple-element.137) | copy-start | bytes 292
  190.1 4.3 %copy-start.16 = (bf16[12,64,256]{2,1,0:T(8,128)(2,1)S(1)}, bf16[12,64,256]{2,1,0:T(8,128)(2,1)}, u32[]{:S(2)}) copy-start(bf16[12,64,256]{2,1,0:T(8,128)(2,1)} %copy-done.15) | copy-start | bytes 1179652
  190.2 4.3 %copy-start.35 = (f32[768]{0:T(1024)S(1)}, f32[768]{0:T(1024)}, u32[]{:S(2)}) copy-start(f32[768]{0:T(1024)} %get-tuple-element.46) | copy-start | bytes 9220
  (20 other events, 24.7 us)

commit v2 on v0

v2 whole, which is shorter than its diff:
```python
import types

import jax
import jax.numpy as jnp
from jax import lax
from jax.experimental import pallas as pl
from jax.experimental.pallas import tpu as pltpu
from jax.sharding import PartitionSpec as P

HD = 64
ROT = 16
WIDE = 768
ROWS = 256
EPS = 1e-05
INV_ROOT_TWO = 0.7071067811865476
INV_ROOT_TWO_PI = 0.3989422804014327
MESH = pl.DeviceIdType.MESH
F32 = jnp.float32
LOW = jnp.bfloat16

UNIT = (48, 48, 48, 192, 16)
WIDTH = (2304, 768, 3072, 768, 768)
CUT = (640, 256, 768, 128, 256)
QKV, OUT, UP, DOWN, SMALL = range(5)
PARTS = 5
GRADS = 4
GROUPS = ((OUT, QKV), (DOWN,), (UP,))
SHARE = 3


def mm(a, b):
    return jnp.dot(a, b, preferred_element_type=F32)


def mm_nt(a, b):
    return lax.dot_general(a, b, (((1,), (1,)), ((), ())), preferred_element_type=F32)


def mm_tn(a, b):
    return lax.dot_general(a, b, (((0,), (0,)), ((), ())), preferred_element_type=F32)


def around(value, shift):
    return lax.rem(value + shift + 4, 4)


def remote(source, target, sent, received, device):
    return pltpu.make_async_remote_copy(
        src_ref=source, dst_ref=target, send_sem=sent, recv_sem=received, device_id=device, device_id_type=MESH
    )


def scratch():
    dma = pltpu.SemaphoreType.DMA
    half = [width // 2 for width in WIDTH]
    own = [UNIT[i] // 2 for i in range(GRADS)] + [16]

    def each(count, shape, dtype=LOW):
        return [pltpu.VMEM(shape(i), dtype) for i in range(count)]

    groups = len(GROUPS)
    return dict(
        mine=each(PARTS, lambda i: (own[i], WIDTH[i]), F32),
        his=each(PARTS, lambda i: (own[i], half[i]), F32),
        unit=each(PARTS, lambda i: (UNIT[i], half[i])),
        full=each(PARTS, lambda i: (16 * UNIT[i], WIDTH[i])),
        total=each(GRADS, lambda i: (16 * UNIT[i], half[i])),
        away=each(GRADS, lambda i: (16 * UNIT[i], half[i])),
        pair=each(GRADS, lambda i: (16 * UNIT[i], half[i])),
        far_b=each(GRADS, lambda i: (4, UNIT[i], half[i])),
        near_b=each(GRADS, lambda i: (8, UNIT[i], half[i])),
        far_a=each(GRADS, lambda i: (UNIT[i], half[i])),
        near_a=each(GRADS, lambda i: (2, UNIT[i], half[i])),
        last=each(GRADS, lambda i: (UNIT[i], half[i]), F32),
        part=pltpu.VMEM((groups, 4 * SHARE, 48, 128), LOW),
        parts_in=pltpu.VMEM((groups, 3, SHARE, 48, 128), LOW),
        whole=pltpu.VMEM((groups, 4 * SHARE, 48, 128), LOW),
        small_grad=pltpu.VMEM((16, WIDE), F32),
        small_in=pltpu.VMEM((10, 16, WIDE), F32),
        small_sum=pltpu.VMEM((3, 16, WIDE), F32),
        vectors=pltpu.VMEM((16, WIDE), F32),
        normal=pltpu.VMEM((ROWS, WIDE), F32),
        inverse=pltpu.VMEM((ROWS, 1), F32),
        valid=pltpu.VMEM((ROWS, 1), F32),
        bias=pltpu.VMEM((ROWS, ROWS), F32),
        turn=pltpu.VMEM((3, ROWS, 128), F32),
        upstream=pltpu.VMEM((ROWS, WIDE), LOW),
        xn1=pltpu.VMEM((ROWS, WIDE), LOW),
        xn2=pltpu.VMEM((ROWS, WIDE), LOW),
        xt=pltpu.VMEM((WIDE, ROWS), LOW),
        qkv=pltpu.VMEM((ROWS, 3 * WIDE), LOW),
        dcontext=pltpu.VMEM((ROWS, WIDE), LOW),
        context=pltpu.VMEM((ROWS, WIDE), LOW),
        dqkv=pltpu.VMEM((ROWS, 3 * WIDE), LOW),
        act=pltpu.VMEM((ROWS, 4 * WIDE), LOW),
        slope=pltpu.VMEM((ROWS, 4 * WIDE), F32),
        dh=pltpu.VMEM((ROWS, 4 * WIDE), LOW),
        dx=pltpu.VMEM((ROWS, WIDE), F32),
        pair_send=dma((PARTS,)),
        pair_recv=dma((PARTS,)),
        send=dma((PARTS, 16)),
        recv=dma((PARTS, 16)),
        near_send=dma((PARTS,)),
        near_recv=dma((PARTS,)),
        keep=dma((PARTS,)),
        swap_send=dma((GRADS,)),
        swap_recv=dma((GRADS,)),
        back_send=dma((GRADS, 16)),
        back_recv=dma((GRADS, 16)),
        z_send=dma((groups, 6)),
        z_recv=dma((groups, 6)),
        small_send=dma((10,)),
        small_recv=dma((10,)),
        out_send=dma((GRADS,)),
        out_recv=dma((GRADS,)),
        out_local=dma((GRADS,)),
    )


KINDS, TREE = jax.tree.flatten(scratch())
SIZES = (72, 96, 24, 24, 24, 24, 24, 24)


def kernel(*refs):
    tokens, cotangent, packed, sequences = refs[:4]
    own = refs[4:8]
    mixed, grad_tokens = refs[8:10]
    outs = refs[10:14]
    small_out = refs[14]
    b = types.SimpleNamespace(**jax.tree.unflatten(TREE, refs[15:]))

    index = lax.axis_index("shard")
    depth = lax.axis_index("replica")
    core = lax.rem(index, 2)
    place = index // 2
    across, along = lax.rem(place, 4), place // 4
    first = across * (1 - core) + along * core
    second = along * (1 - core) + across * core
    stride_a, stride_b = 1 + 3 * core, 4 - 3 * core

    def chip(da, db):
        return around(first, da) * stride_a + around(second, db) * stride_b

    def device(da, db):
        return {"shard": chip(da, db) * 2 + core}

    def deep(dz):
        return {"replica": around(depth, dz)}

    sibling = {"shard": place * 2 + 1 - core}
    started = []

    def start(source, target, sent, received, device_id):
        copy = remote(source, target, sent, received, device_id)
        copy.start()
        started.append(copy)

    def arrived(ref, received):
        remote(ref, ref, b.send.at[0, 0], received, sibling).wait_recv()

    def columns(i, which):
        half = WIDTH[i] // 2
        return pl.ds(pl.multiple_of(which * half, 128), half)

    def block(i, da, db, low=0, high=None):
        u, half = UNIT[i], WIDTH[i] // 2
        high = half if high is None else high
        return b.full[i].at[
            pl.ds(pl.multiple_of(chip(da, db) * u, 16), u),
            pl.ds(pl.multiple_of(core * half + low, 128), high - low),
        ]

    def push(i, slot, source, target, device_id, arrival):
        start(source, target, b.send.at[i, slot], b.recv.at[i, arrival], device_id)

    def hand_over(i, da, db, source=None):
        target = block(i, da, db)
        source = target if source is None else source
        remote(source, target, b.near_send.at[i], b.near_recv.at[i], sibling).start()

    def take(i, slot, ref):
        arrived(ref, b.recv.at[i, slot])

    def swap_own(i):
        start(b.mine[i].at[:, columns(i, 1 - core)], b.his[i], b.pair_send.at[i], b.pair_recv.at[i], sibling)

    def g1(i):
        mine_ref, unit = b.mine[i], b.unit[i]
        arrived(b.his[i], b.pair_recv.at[i])
        half = WIDTH[i] // 2
        mine = jnp.where(core == 0, mine_ref[:, :half], mine_ref[:, half:])
        other = b.his[i][...]
        if i == SMALL:
            unit[...] = (mine + other).astype(LOW)
        else:
            rows = [jnp.where(core == 0, mine, other), jnp.where(core == 0, other, mine)]
            unit[...] = jnp.concatenate(rows, axis=0).astype(LOW)
        here = block(i, 0, 0)
        push(i, 0, unit, here, device(1, 0), 0)
        push(i, 1, unit, here, device(-1, 0), 1)
        push(i, 2, unit, here, device(0, 1), 4)
        push(i, 3, unit, here, device(0, -1), 8)
        hand_over(i, 0, 0, unit)
        pltpu.make_async_copy(unit, here, b.keep.at[i]).start()

    def g2(i):
        half, cut = WIDTH[i] // 2, CUT[i]
        take(i, 0, block(i, -1, 0))
        push(i, 4, block(i, -1, 0, 0, cut), block(i, -1, 0, 0, cut), device(1, 0), 2)
        push(i, 5, block(i, -1, 0), block(i, -1, 0), device(0, 1), 5)
        push(i, 6, block(i, -1, 0), block(i, -1, 0), device(0, -1), 9)
        hand_over(i, -1, 0)
        take(i, 1, block(i, 1, 0))
        push(i, 7, block(i, 1, 0, cut, half), block(i, 1, 0, cut, half), device(-1, 0), 3)
        push(i, 8, block(i, 1, 0), block(i, 1, 0), device(0, 1), 6)
        push(i, 9, block(i, 1, 0), block(i, 1, 0), device(0, -1), 10)
        hand_over(i, 1, 0)

    def g3(i):
        half, cut = WIDTH[i] // 2, CUT[i]
        take(i, 4, block(i, 0, -1))
        push(i, 12, block(i, 0, -1), block(i, 0, -1), device(0, 1), 12)
        hand_over(i, 0, -1)
        take(i, 8, block(i, 0, 1))
        hand_over(i, 0, 1)
        take(i, 2, block(i, 2, 0, 0, cut))
        take(i, 3, block(i, 2, 0, cut, half))
        push(i, 10, block(i, 2, 0), block(i, 2, 0), device(0, 1), 7)
        push(i, 11, block(i, 2, 0), block(i, 2, 0), device(0, -1), 11)
        hand_over(i, 2, 0)

    def g4(i):
        take(i, 5, block(i, -1, -1))
        push(i, 13, block(i, -1, -1), block(i, -1, -1), device(0, 1), 13)
        hand_over(i, -1, -1)
        take(i, 9, block(i, -1, 1))
        hand_over(i, -1, 1)
        take(i, 10, block(i, 1, 1))
        push(i, 14, block(i, 1, 1), block(i, 1, 1), device(0, -1), 14)
        hand_over(i, 1, 1)
        take(i, 6, block(i, 1, -1))
        hand_over(i, 1, -1)

    def g5(i):
        take(i, 11, block(i, 2, 1))
        push(i, 15, block(i, 2, 1), block(i, 2, 1), device(0, -1), 15)
        hand_over(i, 2, 1)
        take(i, 7, block(i, 2, -1))
        hand_over(i, 2, -1)
        take(i, 12, block(i, 0, 2))
        hand_over(i, 0, 2)

    def g6(i):
        for slot, da in ((13, -1), (14, 1), (15, 2)):
            take(i, slot, block(i, da, 2))
            hand_over(i, da, 2)

    def ready(i):
        full = b.full[i]
        mine, other = full.at[:, columns(i, core)], full.at[:, columns(i, 1 - core)]
        remote(mine, other, b.near_send.at[i], b.near_recv.at[i], sibling).wait()
        pltpu.make_async_copy(b.unit[i], block(i, 0, 0), b.keep.at[i]).wait()

    def rows_of(i, where):
        return pl.ds(pl.multiple_of(where * UNIT[i], 16), UNIT[i])

    def in_line(i, a, db):
        return rows_of(i, a * stride_a + around(second, db) * stride_b)

    def back(i, slot, source, target, device_id):
        start(source, target, b.back_send.at[i, slot], b.back_recv.at[i, slot], device_id)

    def back_take(i, slot, ref):
        arrived(ref, b.back_recv.at[i, slot])

    def add_rows(i, where, extra):
        total = b.total[i]
        total[where, :] = (total[where, :].astype(F32) + extra.astype(F32)).astype(LOW)

    def add_pair(i, db):
        for a in range(4):
            where = in_line(i, a, db)
            add_rows(i, where, b.pair[i][where, :])

    def r0(i):
        start(b.away[i], b.pair[i], b.swap_send.at[i], b.swap_recv.at[i], sibling)

    def r1(i):
        total, far, near = b.total[i], b.far_b[i], b.near_b[i]
        arrived(b.pair[i], b.swap_recv.at[i])
        add_pair(i, 2)
        for n, a in enumerate((0, 1, 2, 3)):
            back(i, n, total.at[in_line(i, a, 2), :], far.at[n], device(0, 1 if a < 2 else -1))
        add_pair(i, 1)
        for a in (2, 3):
            back(i, 4 + a, total.at[in_line(i, a, 1), :], near.at[a], device(0, 1))
        add_pair(i, -1)
        for a in (0, 1):
            back(i, 8 + a, total.at[in_line(i, a, -1), :], near.at[4 + a], device(0, -1))

    def r2(i):
        total, far, near = b.total[i], b.far_b[i], b.near_b[i]
        for a in (0, 2, 1, 3):
            db, base = (1, 0) if a < 2 else (-1, 4)
            back_take(i, a, far.at[a])
            add_rows(i, in_line(i, a, db), far[a])
            back(i, 4 + base + a, total.at[in_line(i, a, db), :], near.at[base + a], device(0, db))
        add_pair(i, 0)

    def r3(i):
        half, cut = WIDTH[i] // 2, CUT[i]
        total, near, far = b.total[i], b.near_b[i], b.far_a[i]
        for n in range(8):
            back_take(i, 4 + n, near.at[n])
        for a in range(4):
            where = in_line(i, a, 0)
            value = total[where, :].astype(F32) + near[a].astype(F32) + near[4 + a].astype(F32)
            total[where, :] = value.astype(LOW)
        there = rows_of(i, chip(2, 0))
        low, high = pl.ds(0, cut), pl.ds(cut, half - cut)
        back(i, 12, total.at[there, low], far.at[:, low], device(1, 0))
        back(i, 13, total.at[there, high], far.at[:, high], device(-1, 0))

    def r4(i):
        half, cut = WIDTH[i] // 2, CUT[i]
        total, far, near = b.total[i], b.far_a[i], b.near_a[i]
        for n, cols, da in ((0, pl.ds(0, cut), 1), (1, pl.ds(cut, half - cut), -1)):
            there = rows_of(i, chip(da, 0))
            back_take(i, 12 + n, far.at[:, cols])
            value = total[there, cols].astype(F32) + far[:, cols].astype(F32)
            total[there, cols] = value.astype(LOW)
            back(i, 14 + n, total.at[there, :], near.at[n], device(da, 0))

    def tiles(group):
        n = 0
        for i in GROUPS[group]:
            for r in range(UNIT[i] // 48):
                for t in range(WIDTH[i] // 256):
                    yield n, i, slice(48 * r, 48 * r + 48), slice(128 * t, 128 * t + 128)
                    n += 1

    def share(dz):
        return pl.ds(around(depth, dz) * SHARE, SHARE)

    def z1(group):
        for i in GROUPS[group]:
            near = b.near_a[i]
            back_take(i, 14, near.at[0])
            back_take(i, 15, near.at[1])
            value = b.total[i][rows_of(i, chip(0, 0)), :].astype(F32)
            b.last[i][...] = value + near[0].astype(F32) + near[1].astype(F32)
        part = b.part.at[group]
        for n, i, r, c in tiles(group):
            part[n] = b.last[i][r, c].astype(LOW)
        for n in (1, 0, 2):
            sems = b.z_send.at[group, n], b.z_recv.at[group, n]
            start(part.at[share(n + 1)], b.parts_in.at[group, n], *sems, deep(n + 1))

    def z2(group):
        value = b.part[group, share(0)].astype(F32)
        for n in range(3):
            arrived(b.parts_in.at[group, n], b.z_recv.at[group, n])
            value = value + b.parts_in[group, n].astype(F32)
        whole = b.whole.at[group]
        whole[share(0)] = value.astype(LOW)
        for n in (1, 0, 2):
            sems = b.z_send.at[group, 3 + n], b.z_recv.at[group, 3 + n]
            start(whole.at[share(0)], whole.at[share(0)], *sems, deep(n + 1))

    finals = []

    def z3(group):
        whole = b.whole.at[group]
        for n in range(3):
            arrived(whole.at[share(-n - 1)], b.z_recv.at[group, 3 + n])
        for n, i, r, c in tiles(group):
            b.last[i][r, c] = whole[n].astype(F32)
        for i in GROUPS[group]:
            last, half = b.last[i], UNIT[i] // 2
            target = outs[i].at[:, columns(i, core)]
            copy = remote(
                last.at[pl.ds(pl.multiple_of((1 - core) * half, 8), half), :],
                target,
                b.out_send.at[i],
                b.out_recv.at[i],
                sibling,
            )
            copy.start()
            finals.append(copy)
            copy = pltpu.make_async_copy(
                last.at[pl.ds(pl.multiple_of(core * half, 8), half), :], target, b.out_local.at[i]
            )
            copy.start()
            finals.append(copy)

    rings = ((device(1, 0), device(2, 0), device(-1, 0)), (device(0, 1), device(0, 2), device(0, -1)), tuple(deep(n) for n in (1, 2, 3)))

    def small_send(step):
        source = b.small_grad if step == 0 else b.small_sum.at[step - 1]
        others = (sibling,) if step == 0 else rings[step - 1]
        base = 0 if step == 0 else 3 * step - 2
        for n, target in enumerate(others):
            start(source, b.small_in.at[base + n], b.small_send.at[base + n], b.small_recv.at[base + n], target)

    def small_take(step):
        base, count = (0, 1) if step == 0 else (3 * step - 2, 3)
        value = b.small_grad[...] if step == 0 else b.small_sum[step - 1]
        for n in range(count):
            arrived(b.small_in.at[base + n], b.small_recv.at[base + n])
            value = value + b.small_in[base + n]
        if step == 3:
            small_out[...] = value
        else:
            b.small_sum[step] = value
            small_send(step + 1)

    def lane(rows, width):
        return lax.broadcasted_iota(jnp.int32, (rows, width), 1)

    def place_vectors():
        mine = b.mine[4]
        mine[...] = jnp.zeros_like(mine)
        row, offset = 0, 0
        for size in SIZES:
            width = 32 * size
            line = jnp.concatenate([packed[0:1, :], jnp.zeros((1, width - 384), F32)], axis=1)
            line = jnp.broadcast_to(line, (8, width))
            line = pltpu.roll(line, lax.rem(index * size - offset + width, width), 1)
            at = lane(8, width)
            line = jnp.where((at >= index * size) & (at < index * size + size), line, 0.0)
            for r in range(width // WIDE):
                mine[row : row + 1, :] = line[0:1, WIDE * r : WIDE * r + WIDE]
                row += 1
            offset += size

    def prepare():
        x = tokens[...].astype(F32)
        centered = x - jnp.mean(x, axis=-1, keepdims=True)
        inverse = lax.rsqrt(jnp.mean(centered * centered, axis=-1, keepdims=True) + EPS)
        b.normal[...] = centered * inverse
        b.inverse[...] = inverse
        slot = lax.broadcasted_iota(jnp.int32, (ROWS, ROWS), 0)
        offsets = sequences[2:3, :]
        inside = (sequences[0:1, :] == index * 4 + depth) & (slot >= offsets) & (slot < offsets + sequences[1:2, :])
        ones = jnp.where(inside, 1.0, 0.0)
        valid = jnp.sum(ones, axis=1, keepdims=True)
        b.valid[...] = valid
        position = jnp.sum(jnp.where(inside, (slot - offsets).astype(F32), 0.0), axis=1, keepdims=True)
        rest = jnp.where(lane(ROWS, 128) == 0, 1.0 - valid, 0.0)
        member = jnp.concatenate([ones, rest], axis=1).astype(LOW)
        same = mm_nt(member, member)
        b.bias[...] = jnp.where((same > 0.5) & (lane(ROWS, ROWS) <= slot), 0.0, -1e30)
        at = lane(1, 128)
        freq = jnp.zeros((1, 128), F32)
        for n in range(ROT // 2):
            freq = jnp.where((at & 7) == n, 10000.0 ** (-2.0 * n / ROT), freq)
        angle = position * freq
        within = lane(ROWS, 128) & (HD - 1)
        sine = jnp.sin(angle)
        turn = b.turn
        turn[0] = jnp.where(within < ROT, jnp.cos(angle), 1.0)
        turn[1] = jnp.where(within < ROT // 2, -sine, 0.0)
        turn[2] = jnp.where((within >= ROT // 2) & (within < ROT), sine, 0.0)
        upstream = cotangent[...].astype(F32) * valid
        b.upstream[...] = upstream.astype(LOW)
        grads = b.small_grad
        grads[...] = jnp.zeros_like(grads)
        grads[7:8, :] = jnp.sum(upstream, axis=0, keepdims=True)

    def rotate(value, sign):
        turn = b.turn
        moved = pltpu.roll(value, 120, 1) * turn[1] + pltpu.roll(value, 8, 1) * turn[2]
        return value * turn[0] + moved if sign > 0 else value * turn[0] - moved

    def vector(row, low=0, size=WIDE):
        return b.vectors[row : row + 1, low : low + size]

    def norms():
        values = jnp.sum(b.full[4][...].astype(F32).reshape(16, 16, WIDE), axis=0)
        b.vectors[...] = values
        normal = b.normal[...]
        one = (normal * vector(9) + vector(10)).astype(LOW)
        b.xn1[...] = one
        b.xt[...] = one.T
        b.xn2[...] = (normal * vector(11) + vector(12)).astype(LOW)

    def project(t):
        value = mm(b.xn1[...], b.full[0][:, 256 * t : 256 * t + 256]) + vector(t // 3, 256 * (t % 3), 256)
        for n in range(2):
            part = value[:, 128 * n : 128 * n + 128]
            if t < 6:
                part = rotate(part, 1).astype(LOW)
            if t < 3:
                part = part.astype(F32) * HD ** (-0.5)
            b.qkv[:, 256 * t + 128 * n : 256 * t + 128 * n + 128] = part.astype(LOW)

    def context_back():
        b.dcontext[...] = mm_nt(b.upstream[...], b.full[1][...]).astype(LOW)

    def heads(p):
        cols = slice(128 * p, 128 * p + 128)
        q = b.qkv[:, 128 * p : 128 * p + 128]
        k = b.qkv[:, WIDE + 128 * p : WIDE + 128 * p + 128]
        v = b.qkv[:, 2 * WIDE + 128 * p : 2 * WIDE + 128 * p + 128]
        dc = b.dcontext[:, cols]
        lower = lane(ROWS, 128) < HD
        results = []
        for h in range(2):
            mask = jnp.where(lower if h == 0 else ~lower, 1.0, 0.0).astype(LOW)
            scores = mm_nt(q * mask, k) + b.bias[...]
            e = jnp.exp(scores - jnp.max(scores, axis=-1, keepdims=True))
            soft = e * (1.0 / jnp.sum(e, axis=-1, keepdims=True))
            probs = soft.astype(LOW)
            dprobs = mm_nt(dc * mask, v)
            ds = (soft * (dprobs - jnp.sum(soft * dprobs, axis=-1, keepdims=True))).astype(LOW)
            results.append((mm(probs, v), mm_tn(probs, dc), mm(ds, k), mm_tn(ds, q)))
        context, dv, dq, dk = (jnp.where(lower, one, two) for one, two in zip(*results))
        b.context[:, cols] = context.astype(LOW)
        dq = rotate(dq * HD ** (-0.5), -1).astype(LOW)
        dk = rotate(dk, -1).astype(LOW)
        dv = dv.astype(LOW)
        for n, value in enumerate((dq, dk, dv)):
            b.dqkv[:, WIDE * n + 128 * p : WIDE * n + 128 * p + 128] = value
            total = jnp.sum(value.astype(F32), axis=0, keepdims=True)
            b.small_grad[n : n + 1, cols] = total

    def grad_out():
        turned = b.context[...].T
        b.away[1][...] = mm(turned, b.upstream[:, columns(OUT, 1 - core)]).astype(LOW)
        b.total[1][...] = mm(turned, b.upstream[:, columns(OUT, core)]).astype(LOW)

    def grad_wide(i, source, which, target):
        step = 384
        for t in range(WIDTH[i] // 2 // step):
            at = pl.multiple_of(which * (WIDTH[i] // 2) + step * t, 128)
            target[:, step * t : step * t + step] = mm(b.xt[...], source[:, pl.ds(at, step)]).astype(LOW)

    def hidden(t):
        cols = slice(512 * t, 512 * t + 512)
        h = mm(b.xn2[...], b.full[2][:, cols])
        at = 512 * t
        pieces = []
        for n in range(2):
            pieces.append(vector(3 + (at + 256 * n) // WIDE, (at + 256 * n) % WIDE, 256))
        h = h + jnp.concatenate(pieces, axis=1)
        cdf = 0.5 * (1.0 + lax.erf(h * INV_ROOT_TWO))
        b.act[:, cols] = (h * cdf).astype(LOW)
        b.slope[:, cols] = cdf + h * jnp.exp(-0.5 * h * h) * INV_ROOT_TWO_PI

    def grad_down(t):
        rows = slice(512 * t, 512 * t + 512)
        turned = b.act[:, rows].T
        b.away[3][rows, :] = mm(turned, b.upstream[:, columns(DOWN, 1 - core)]).astype(LOW)
        b.total[3][rows, :] = mm(turned, b.upstream[:, columns(DOWN, core)]).astype(LOW)

    def hidden_back(t):
        cols = slice(512 * t, 512 * t + 512)
        value = (mm_nt(b.upstream[...], b.full[3][cols, :]) * b.slope[:, cols]).astype(LOW)
        b.dh[:, cols] = value
        total = jnp.sum(value.astype(F32), axis=0, keepdims=True)
        for n in range(2):
            at = 512 * t + 256 * n
            row, low = 3 + at // WIDE, at % WIDE
            b.small_grad[row : row + 1, low : low + 256] = total[:, 256 * n : 256 * n + 256]

    def turn_xn2():
        b.xt[...] = b.xn2[...].T

    def finish_forward():
        value = mm(b.context[...], b.full[1][...]) + mm(b.act[...], b.full[3][...])
        value = value + (vector(7) + vector(8)) + tokens[...].astype(F32)
        mixed[...] = (value * b.valid[...]).astype(LOW)

    def norm_back(upstream, gain, row):
        normal = b.normal[...]
        b.small_grad[row : row + 1, :] = jnp.sum(upstream * normal, axis=0, keepdims=True)
        b.small_grad[row + 1 : row + 2, :] = jnp.sum(upstream, axis=0, keepdims=True)
        scaled = upstream * gain
        centre = jnp.mean(scaled, axis=-1, keepdims=True)
        slope = jnp.mean(scaled * normal, axis=-1, keepdims=True)
        return b.inverse[...] * (scaled - centre - normal * slope)

    def back_one():
        grad = mm_nt(b.dqkv[...], b.full[0][...])
        b.dx[...] = b.upstream[...].astype(F32) + norm_back(grad, vector(9), 8)

    def back_two():
        grad = mm_nt(b.dh[...], b.full[2][...])
        grad_tokens[...] = (b.dx[...] + norm_back(grad, vector(11), 10)).astype(LOW)

    for i in range(GRADS):
        b.mine[i][...] = own[i][...].astype(F32)
    place_vectors()
    targets = [device(1, 0), device(-1, 0), device(2, 0), device(0, 1), device(0, -1), device(0, 2), sibling]
    targets += [deep(1), deep(2), deep(3)]
    barrier = pltpu.get_barrier_semaphore()
    for target in targets:
        pl.semaphore_signal(barrier, inc=1, device_id=target, device_id_type=MESH)
    pl.semaphore_wait(barrier, len(targets))

    attention = (SMALL, QKV, OUT)
    for i in (SMALL, QKV, OUT, UP, DOWN):
        swap_own(i)
    for i in (SMALL, QKV, OUT, UP, DOWN):
        g1(i)
    prepare()
    for step in (g2, g3):
        for i in (SMALL, QKV, OUT, UP, DOWN):
            step(i)
    for step in (g4, g5, g6):
        for i in attention:
            step(i)
        if step is not g6:
            step(UP)
            step(DOWN)
    ready(SMALL)
    norms()
    ready(QKV)
    for t in range(9):
        project(t)
    ready(OUT)
    context_back()
    g6(UP)
    heads(0)
    g6(DOWN)
    for p in range(1, 6):
        heads(p)
    grad_out()
    r0(OUT)
    grad_wide(QKV, b.dqkv, 1 - core, b.away[0])
    r0(QKV)
    r1(OUT)
    grad_wide(QKV, b.dqkv, core, b.total[0])
    r1(QKV)
    ready(UP)
    for t in range(6):
        hidden(t)
        if t == 2:
            r2(OUT)
    for t in range(6):
        grad_down(t)
    r0(DOWN)
    r2(QKV)
    turn_xn2()
    ready(DOWN)
    r1(DOWN)
    for t in range(6):
        hidden_back(t)
    grad_wide(UP, b.dh, 1 - core, b.away[2])
    r0(UP)
    grad_wide(UP, b.dh, core, b.total[2])
    r1(UP)
    r3(OUT)
    r3(QKV)
    r2(DOWN)
    back_one()
    r2(UP)
    r4(OUT)
    r4(QKV)
    back_two()
    small_send(0)
    r3(DOWN)
    z1(0)
    small_take(0)
    r3(UP)
    r4(DOWN)
    finish_forward()
    small_take(1)
    z2(0)
    r4(UP)
    z1(1)
    small_take(2)
    z1(2)
    z3(0)
    z2(1)
    z2(2)
    small_take(3)
    z3(1)
    z3(2)
    for copy in finals:
        copy.wait()
    for copy in started:
        copy.wait_send()


VECTORS = ((0, 72), (7, 24), (3, 96), (7, 24), (8, 24), (9, 24), (10, 24), (11, 24))


def deliver(*refs):
    count = 2 + GRADS
    sums = refs[count]
    ends = refs[count + 1 : 2 * count + 1]
    parts = refs[2 * count + 1 :]
    for n in range(count):
        ends[n][...] = refs[n][...]
    index = lax.axis_index("shard")
    for (row, size), part in zip(VECTORS, parts):
        width = 32 * size
        line = jnp.concatenate([sums[row + r : row + r + 1, :] for r in range(width // WIDE)], axis=1)
        line = pltpu.roll(jnp.broadcast_to(line, (8, width)), lax.rem(width - index * size, width), 1)
        part[...] = line[0:1, :size]


def per_device(
    tokens,
    cotangent,
    w_qkv,
    b_qkv,
    w_out,
    b_out,
    w_up,
    b_up,
    w_down,
    b_down,
    ln1_gain,
    ln1_bias,
    ln2_gain,
    ln2_bias,
    seq_device,
    seq_lengths,
    seq_offsets,
):
    index = lax.axis_index("shard")
    packed = jnp.concatenate(
        [b_qkv, b_up, b_out, b_down, ln1_gain, ln1_bias, ln2_gain, ln2_bias, jnp.zeros((72,), LOW)]
    ).astype(F32)
    packed = jnp.broadcast_to(packed[None, :], (8, 384))
    sequences = jnp.stack([seq_device, seq_lengths, seq_offsets] + [seq_device] * 5)
    vmem = pl.BlockSpec(memory_space=pltpu.VMEM)
    anywhere = pl.BlockSpec(memory_space=pl.ANY)
    rows = jax.ShapeDtypeStruct((ROWS, WIDE), LOW)
    shapes = [rows, rows] + [jax.ShapeDtypeStruct((UNIT[i] // 2, WIDTH[i]), F32) for i in range(GRADS)]
    results = pl.pallas_call(
        kernel,
        out_shape=shapes + [jax.ShapeDtypeStruct((16, WIDE), F32)],
        in_specs=[vmem] * 8,
        out_specs=[vmem] * 2 + [anywhere] * GRADS + [vmem],
        scratch_shapes=KINDS,
        compiler_params=pltpu.CompilerParams(
            collective_id=0, has_side_effects=True, vmem_limit_bytes=63 * 1024 * 1024
        ),
    )(tokens, cotangent, packed, sequences, w_qkv, w_out, w_up, w_down)
    results = pl.pallas_call(
        deliver,
        out_shape=shapes + [jax.ShapeDtypeStruct((1, size), F32) for _, size in VECTORS],
        in_specs=[vmem] * 7,
        out_specs=[vmem] * (6 + len(VECTORS)),
    )(*results)
    mixed, grad_tokens, out_qkv, out_out, out_up, out_down = results[:6]
    b_qkv, b_out, b_up, b_down, gain1, bias1, gain2, bias2 = (value.reshape(-1) for value in results[6:])
    return (
        mixed,
        grad_tokens,
        out_qkv,
        b_qkv,
        out_out,
        b_out,
        out_up,
        b_up,
        out_down,
        b_down,
        gain1,
        bias1,
        gain2,
        bias2,
    )


def solution(mesh):
    return jax.shard_map(
        per_device,
        mesh=mesh,
        in_specs=(
            P(("shard", "replica"), None),
            P(("shard", "replica"), None),
            P("shard", None),
            P("shard"),
            P("shard", None),
            P("shard"),
            P("shard", None),
            P("shard"),
            P("shard", None),
            P("shard"),
            P("shard"),
            P("shard"),
            P("shard"),
            P("shard"),
            P(),
            P(),
            P(),
        ),
        out_specs=(
            P(("shard", "replica"), None),
            P(("shard", "replica"), None),
            P("shard", None),
            P("shard"),
            P("shard", None),
            P("shard"),
            P("shard", None),
            P("shard"),
            P("shard", None),
            P("shard"),
            P("shard"),
            P("shard"),
            P("shard"),
            P("shard"),
        ),
        check_vma=False,
    )
```

time: 593 us -> 127 us (0.21)
  blocking collectives: 261 us -> 0 us
  waiting for transfers between devices: 218 us -> 0 us
  Pallas kernels: 0 us -> 123 us
  matrix products: 50.1 us -> 0 us
  other arithmetic: 20.9 us -> 0 us
  local copies, waits for them, and re-layouts: 22.1 us -> 2.62 us
  between operations: 18.5 us -> 0.91 us
    unnamed x2 -> x0, blocking collectives: 246 us -> none
    reduce_scatter x4 -> x0, waiting for transfers between devices: 168 us -> none  [the longest x1 87.1 us: per_device(): lax.psum_scatter(grad_w_down.astype(jnp.bfloat16), 'shard', scatter_dimen...]
    pallas_call x0 -> x2, Pallas kernels: none -> 123 us  [the longest x1 121 us: per_device(): pl.pallas_call(kernel, out_shape=shapes + [jax.ShapeDtypeStruct((16, WIDE...]
    dot_general x18 -> x0, matrix products: 50.1 us -> none  [the longest x1 6.15 us: per_device(): jnp.dot(xn2, wu_all, preferred_element_type=jnp.float32)]
    psum x1 -> x0, waiting for transfers between devices: 23.8 us -> none  [per_device(): lax.psum(shares[0].astype(jnp.bfloat16), 'replica').astype(jnp.float32)]
    all_gather x4 -> x0, waiting for transfers between devices: 23.2 us -> none  [the longest x1 23.2 us: per_device(): lax.all_gather(w_down, 'shard', axis=0, tiled=True)]
    unnamed x115 -> x22, local copies, waits for them, and re-layouts: 18.1 us -> 1.3 us
    psum x1 -> x0, blocking collectives: 14.3 us -> none  [per_device(): lax.psum(shares[1].astype(jnp.bfloat16), 'replica').astype(jnp.float32)]
  transfers between devices with their start and end apart: 9 -> 0, of which waited for: 5 -> 0; matrix products, arithmetic and copies ran while one was open for 14% -> 0% of each run, Pallas kernels for 0% -> 0%
where the time goes in v2:
time: 127 us
  Pallas kernels  123 us (97%)
  local copies, waits for them, and re-layouts  2.62 us (2%)
    pallas_call x1, Pallas kernels, per_device(): pl.pallas_call(kernel, out_shape=shapes + [jax.ShapeDtypeStruct((16, WIDE...  121 us
    pallas_call x1, Pallas kernels, per_device(): pl.pallas_call(deliver, out_shape=shapes + [jax.ShapeDtypeStruct((1, size...  2.73 us

profile of v2, /device:TPU:1, one launch (start us, length us, event | category | flops | bytes accessed | tf_op | source)
XLA Modules:
  0.0 126.8 jit_solution(16182246648836099916)
XLA Ops:
  0.6 0.0 copy-start.10
  0.7 0.0 copy-start.6
  0.7 0.0 copy-start.7
  0.7 0.0 copy-start.8
  0.7 0.0 copy-start.9
  0.7 0.0 copy-start.3
  0.7 0.0 copy-start.4
  0.7 0.0 copy-start.5
  0.7 0.6 copy-done.10
  1.3 0.0 copy-done.6
  1.3 0.0 copy-done.7
  1.3 0.0 copy-done.8
  1.4 0.0 copy-done.9
  1.4 0.0 copy-done.3
  1.4 0.0 copy-done.4
  1.4 0.0 copy-done.5
  1.4 0.0 copy-start
  1.4 0.0 copy-start.1
  1.4 0.0 copy-start.2
  1.4 0.1 concatenate.7
  1.5 0.6 copy-done
  2.1 0.0 copy-done.1
  2.1 0.0 copy-done.2
  2.1 0.6 stack.20.refs_3_
  2.7 0.6 broadcast_in_dim.10.refs_2_
  3.3 120.5 %shard_map.272 = (bf16[256,768]{1,0:T(8,128)(2,1)}, bf16[256,768]{1,0:T(8,128)(2,1)}, f32[24,2304]{1,0:T(8,128)}, f32[24,768]{1,0:T(8,128)}, f32[24,3072]{1,0:T(...) custom-call(bf16[256,768]{1,0:T(8,128)(2,1)} %refs_0_.1, bf16[256,768]{1,0:T(8,128)(2,1)} %refs_1_.1, ...), custom_call_target="tpu_custom_call" | custom-call | tf_op jit(solution)/shard_map/pallas_call | solution.py:733
  123.9 2.7 %shard_map.273 = (bf16[256,768]{1,0:T(8,128)(2,1)}, bf16[256,768]{1,0:T(8,128)(2,1)}, f32[24,2304]{1,0:T(8,128)}, f32[24,768]{1,0:T(8,128)}, f32[24,3072]{1,0:T(...) custom-call(bf16[256,768]{1,0:T(8,128)(2,1)} %get-tuple-element.35.r, ...), custom_call_target="tpu_custom_call" | custom-call | tf_op jit(solution)/shard_map/pallas_call | solution.py:743
  (1 shorter events, 0.0 us)
Async XLA Ops:
  0.6 0.7 copy-start.10
  0.7 0.7 copy-start.6
  0.7 0.7 copy-start.7
  0.7 0.7 copy-start.8
  0.7 0.7 copy-start.9
  0.7 0.7 copy-start.3
  0.7 0.7 copy-start.4
  0.7 0.7 copy-start.5
  1.4 0.7 copy-start
  1.4 0.7 copy-start.1
  1.4 0.7 copy-start.2

commit v3 on v2

--- a/solution.py
+++ b/solution.py
@@ -24,7 +24,7 @@
 QKV, OUT, UP, DOWN, SMALL = range(5)
 PARTS = 5
 GRADS = 4
-GROUPS = ((OUT, QKV), (DOWN,), (UP,))
+GROUPS = ((OUT, QKV), (UP,))
 SHARE = 3
 
 
@@ -64,13 +64,17 @@
         his=each(PARTS, lambda i: (own[i], half[i]), F32),
         unit=each(PARTS, lambda i: (UNIT[i], half[i])),
         full=each(PARTS, lambda i: (16 * UNIT[i], WIDTH[i])),
-        total=each(GRADS, lambda i: (16 * UNIT[i], half[i])),
-        away=each(GRADS, lambda i: (16 * UNIT[i], half[i])),
-        pair=each(GRADS, lambda i: (16 * UNIT[i], half[i])),
-        far_b=each(GRADS, lambda i: (4, UNIT[i], half[i])),
-        near_b=each(GRADS, lambda i: (8, UNIT[i], half[i])),
-        far_a=each(GRADS, lambda i: (UNIT[i], half[i])),
-        near_a=each(GRADS, lambda i: (2, UNIT[i], half[i])),
+        total=each(GRADS, lambda i: (16, 4, 48, half[i]) if i == DOWN else (16 * UNIT[i], half[i])),
+        away=each(GRADS, lambda i: (16, 4, 48, half[i]) if i == DOWN else (16 * UNIT[i], half[i])),
+        pair=each(GRADS, lambda i: (16, 4, 48, half[i]) if i == DOWN else (16 * UNIT[i], half[i])),
+        far_b=each(DOWN, lambda i: (4, 48, half[i])),
+        near_b=each(GRADS, lambda i: (12 if i == DOWN else 8, 48, half[i])),
+        near_a=each(GRADS, lambda i: (3, 48, half[i])),
+        deep_far=pltpu.VMEM((2, 8, 48, 384), LOW),
+        deep_near=pltpu.VMEM((2, 16, 48, 384), LOW),
+        deep_last=pltpu.VMEM((4, 48, 384), LOW),
+        down_send=dma((9,)),
+        down_recv=dma((9,)),
         last=each(GRADS, lambda i: (UNIT[i], half[i]), F32),
         part=pltpu.VMEM((groups, 4 * SHARE, 48, 128), LOW),
         parts_in=pltpu.VMEM((groups, 3, SHARE, 48, 128), LOW),
@@ -264,8 +268,13 @@
     def rows_of(i, where):
         return pl.ds(pl.multiple_of(where * UNIT[i], 16), UNIT[i])
 
-    def in_line(i, a, db):
-        return rows_of(i, a * stride_a + around(second, db) * stride_b)
+    def in_line(a, db):
+        return a * stride_a + around(second, db) * stride_b
+
+    def cell(i, where, cols=slice(None)):
+        if i == DOWN:
+            return b.total[i].at[where, depth, :, cols]
+        return b.total[i].at[rows_of(i, where), cols]
 
     def back(i, slot, source, target, device_id):
         start(source, target, b.back_send.at[i, slot], b.back_recv.at[i, slot], device_id)
@@ -273,63 +282,115 @@
     def back_take(i, slot, ref):
         arrived(ref, b.back_recv.at[i, slot])
 
-    def add_rows(i, where, extra):
-        total = b.total[i]
-        total[where, :] = (total[where, :].astype(F32) + extra.astype(F32)).astype(LOW)
-
     def add_pair(i, db):
         for a in range(4):
-            where = in_line(i, a, db)
-            add_rows(i, where, b.pair[i][where, :])
+            where = rows_of(i, in_line(a, db))
+            b.total[i][where, :] = b.total[i][where, :] + b.pair[i][where, :]
 
     def r0(i):
         start(b.away[i], b.pair[i], b.swap_send.at[i], b.swap_recv.at[i], sibling)
 
     def r1(i):
-        total, far, near = b.total[i], b.far_b[i], b.near_b[i]
+        near = b.near_b[i]
+        if i == DOWN:
+            for n, db in enumerate((2, 1, -1)):
+                for a in range(4):
+                    back(i, 4 * n + a, cell(i, in_line(a, db)), near.at[4 * n + a], device(0, db))
+            return
         arrived(b.pair[i], b.swap_recv.at[i])
         add_pair(i, 2)
-        for n, a in enumerate((0, 1, 2, 3)):
-            back(i, n, total.at[in_line(i, a, 2), :], far.at[n], device(0, 1 if a < 2 else -1))
+        for a in range(4):
+            back(i, a, cell(i, in_line(a, 2)), b.far_b[i].at[a], device(0, 1 if a < 2 else -1))
         add_pair(i, 1)
         for a in (2, 3):
-            back(i, 4 + a, total.at[in_line(i, a, 1), :], near.at[a], device(0, 1))
+            back(i, 4 + a, cell(i, in_line(a, 1)), near.at[a], device(0, 1))
         add_pair(i, -1)
         for a in (0, 1):
-            back(i, 8 + a, total.at[in_line(i, a, -1), :], near.at[4 + a], device(0, -1))
+            back(i, 8 + a, cell(i, in_line(a, -1)), near.at[4 + a], device(0, -1))
 
     def r2(i):
-        total, far, near = b.total[i], b.far_b[i], b.near_b[i]
+        far, near = b.far_b[i], b.near_b[i]
         for a in (0, 2, 1, 3):
             db, base = (1, 0) if a < 2 else (-1, 4)
+            here = cell(i, in_line(a, db))
             back_take(i, a, far.at[a])
-            add_rows(i, in_line(i, a, db), far[a])
-            back(i, 4 + base + a, total.at[in_line(i, a, db), :], near.at[base + a], device(0, db))
+            here[...] = here[...] + far[a]
+            back(i, 4 + base + a, here, near.at[base + a], device(0, db))
         add_pair(i, 0)
 
     def r3(i):
-        half, cut = WIDTH[i] // 2, CUT[i]
-        total, near, far = b.total[i], b.near_b[i], b.far_a[i]
-        for n in range(8):
-            back_take(i, 4 + n, near.at[n])
+        near = b.near_b[i]
+        first_slot, lines = (0, 3) if i == DOWN else (4, 2)
+        for n in range(4 * lines):
+            back_take(i, first_slot + n, near.at[n])
         for a in range(4):
-            where = in_line(i, a, 0)
-            value = total[where, :].astype(F32) + near[a].astype(F32) + near[4 + a].astype(F32)
-            total[where, :] = value.astype(LOW)
-        there = rows_of(i, chip(2, 0))
-        low, high = pl.ds(0, cut), pl.ds(cut, half - cut)
-        back(i, 12, total.at[there, low], far.at[:, low], device(1, 0))
-        back(i, 13, total.at[there, high], far.at[:, high], device(-1, 0))
-
-    def r4(i):
-        half, cut = WIDTH[i] // 2, CUT[i]
-        total, far, near = b.total[i], b.far_a[i], b.near_a[i]
-        for n, cols, da in ((0, pl.ds(0, cut), 1), (1, pl.ds(cut, half - cut), -1)):
-            there = rows_of(i, chip(da, 0))
-            back_take(i, 12 + n, far.at[:, cols])
-            value = total[there, cols].astype(F32) + far[:, cols].astype(F32)
-            total[there, cols] = value.astype(LOW)
-            back(i, 14 + n, total.at[there, :], near.at[n], device(da, 0))
+            here = cell(i, in_line(a, 0))
+            value = here[...].astype(F32)
+            for n in range(lines):
+                value = value + near[4 * n + a].astype(F32)
+            here[...] = value.astype(LOW)
+        for n, da in enumerate((2, 1, -1)):
+            back(i, 12 + n, cell(i, chip(da, 0)), b.near_a[i].at[n], device(da, 0))
+
+    def r5(i):
+        near = b.near_a[i]
+        value = cell(i, chip(0, 0))[...].astype(F32)
+        for n in range(3):
+            back_take(i, 12 + n, near.at[n])
+            value = value + near[n].astype(F32)
+        return value
+
+    def pieces(part, dz):
+        return b.total[DOWN].at[8 * part : 8 * part + 8, around(depth, dz)]
+
+    def down(slot, source, target, dz):
+        start(source, target, b.down_send.at[slot], b.down_recv.at[slot], deep(dz))
+
+    def e1():
+        arrived(b.pair[DOWN], b.swap_recv.at[DOWN])
+        near = b.deep_near
+        for dz in (2, 1, -1, 0):
+            at = around(depth, dz)
+            b.total[DOWN][:, at] = b.total[DOWN][:, at] + b.pair[DOWN][:, at]
+            if dz == 2:
+                down(0, pieces(0, 2), b.deep_far.at[0], 1)
+                down(1, pieces(1, 2), b.deep_far.at[1], -1)
+            elif dz == 1:
+                down(2, pieces(1, 1), near.at[0, 8:16], 1)
+            elif dz == -1:
+                down(3, pieces(0, -1), near.at[1, 0:8], -1)
+
+    def e2():
+        for part, dz in ((0, 1), (1, -1)):
+            here = pieces(part, dz)
+            arrived(b.deep_far.at[part], b.down_recv.at[part])
+            here[...] = here[...] + b.deep_far[part]
+            down(4 + part, here, b.deep_near.at[part, 8 * part : 8 * part + 8], dz)
+
+    def e3():
+        near = b.deep_near
+        for part in range(2):
+            arrived(near.at[0, 8 * part : 8 * part + 8], b.down_recv.at[4 if part == 0 else 2])
+            arrived(near.at[1, 8 * part : 8 * part + 8], b.down_recv.at[3 if part == 0 else 5])
+            here = pieces(part, 0)
+            value = here[...].astype(F32)
+            for n in range(2):
+                value = value + near[n, 8 * part : 8 * part + 8].astype(F32)
+            here[...] = value.astype(LOW)
+
+    def e4():
+        last = b.deep_last
+        last[depth] = r5(DOWN).astype(LOW)
+        for n in (1, 0, 2):
+            down(6 + n, last.at[depth], last.at[depth], n + 1)
+
+    def e5():
+        last = b.deep_last
+        for n in range(3):
+            arrived(last.at[around(depth, -n - 1)], b.down_recv.at[6 + n])
+        for n in range(4):
+            b.last[DOWN][48 * n : 48 * n + 48, :] = last[n].astype(F32)
+        hand_out(DOWN)
 
     def tiles(group):
         n = 0
@@ -344,11 +405,7 @@
 
     def z1(group):
         for i in GROUPS[group]:
-            near = b.near_a[i]
-            back_take(i, 14, near.at[0])
-            back_take(i, 15, near.at[1])
-            value = b.total[i][rows_of(i, chip(0, 0)), :].astype(F32)
-            b.last[i][...] = value + near[0].astype(F32) + near[1].astype(F32)
+            b.last[i][...] = r5(i)
         part = b.part.at[group]
         for n, i, r, c in tiles(group):
             part[n] = b.last[i][r, c].astype(LOW)
@@ -376,22 +433,20 @@
         for n, i, r, c in tiles(group):
             b.last[i][r, c] = whole[n].astype(F32)
         for i in GROUPS[group]:
-            last, half = b.last[i], UNIT[i] // 2
-            target = outs[i].at[:, columns(i, core)]
-            copy = remote(
-                last.at[pl.ds(pl.multiple_of((1 - core) * half, 8), half), :],
-                target,
-                b.out_send.at[i],
-                b.out_recv.at[i],
-                sibling,
-            )
-            copy.start()
-            finals.append(copy)
-            copy = pltpu.make_async_copy(
-                last.at[pl.ds(pl.multiple_of(core * half, 8), half), :], target, b.out_local.at[i]
-            )
-            copy.start()
-            finals.append(copy)
+            hand_out(i)
+
+    def hand_out(i):
+        last, half = b.last[i], UNIT[i] // 2
+        target = outs[i].at[:, columns(i, core)]
+        copy = remote(
+            last.at[pl.ds(pl.multiple_of((1 - core) * half, 8), half), :], target, b.out_send.at[i], b.out_recv.at[i], sibling
+        )
+        copy.start()
+        finals.append(copy)
+        source = last.at[pl.ds(pl.multiple_of(core * half, 8), half), :]
+        copy = pltpu.make_async_copy(source, target, b.out_local.at[i])
+        copy.start()
+        finals.append(copy)
 
     rings = ((device(1, 0), device(2, 0), device(-1, 0)), (device(0, 1), device(0, 2), device(0, -1)), tuple(deep(n) for n in (1, 2, 3)))
 
@@ -548,10 +603,10 @@
         b.slope[:, cols] = cdf + h * jnp.exp(-0.5 * h * h) * INV_ROOT_TWO_PI
 
     def grad_down(t):
-        rows = slice(512 * t, 512 * t + 512)
-        turned = b.act[:, rows].T
-        b.away[3][rows, :] = mm(turned, b.upstream[:, columns(DOWN, 1 - core)]).astype(LOW)
-        b.total[3][rows, :] = mm(turned, b.upstream[:, columns(DOWN, core)]).astype(LOW)
+        turned = b.act[:, 768 * t : 768 * t + 768].T
+        for target, which in ((b.away[DOWN], 1 - core), (b.total[DOWN], core)):
+            value = mm(turned, b.upstream[:, columns(DOWN, which)]).astype(LOW)
+            target[4 * t : 4 * t + 4] = value.reshape(4, 4, 48, 384)
 
     def hidden_back(t):
         cols = slice(512 * t, 512 * t + 512)
@@ -588,43 +643,55 @@
         grad = mm_nt(b.dh[...], b.full[2][...])
         grad_tokens[...] = (b.dx[...] + norm_back(grad, vector(11), 10)).astype(LOW)
 
-    for i in range(GRADS):
-        b.mine[i][...] = own[i][...].astype(F32)
-    place_vectors()
     targets = [device(1, 0), device(-1, 0), device(2, 0), device(0, 1), device(0, -1), device(0, 2), sibling]
     targets += [deep(1), deep(2), deep(3)]
     barrier = pltpu.get_barrier_semaphore()
     for target in targets:
         pl.semaphore_signal(barrier, inc=1, device_id=target, device_id_type=MESH)
+    for i in range(GRADS):
+        b.mine[i][...] = own[i][...].astype(F32)
     pl.semaphore_wait(barrier, len(targets))
-
-    attention = (SMALL, QKV, OUT)
-    for i in (SMALL, QKV, OUT, UP, DOWN):
+    for i in (QKV, OUT, UP, DOWN):
         swap_own(i)
-    for i in (SMALL, QKV, OUT, UP, DOWN):
+    place_vectors()
+    swap_own(SMALL)
+    attention = (QKV, SMALL, OUT)
+    for i in (QKV, SMALL, OUT, UP, DOWN):
         g1(i)
     prepare()
     for step in (g2, g3):
-        for i in (SMALL, QKV, OUT, UP, DOWN):
-            step(i)
-    for step in (g4, g5, g6):
         for i in attention:
             step(i)
-        if step is not g6:
-            step(UP)
-            step(DOWN)
+    g2(UP)
+    for i in attention:
+        g4(i)
+    g2(DOWN)
+    g3(UP)
+    for i in attention:
+        g5(i)
+    g4(UP)
+    for i in attention:
+        g6(i)
     ready(SMALL)
     norms()
     ready(QKV)
     for t in range(9):
         project(t)
+        if t == 1:
+            g5(UP)
+        if t == 4:
+            g3(DOWN)
     ready(OUT)
     context_back()
     g6(UP)
     heads(0)
-    g6(DOWN)
-    for p in range(1, 6):
-        heads(p)
+    g4(DOWN)
+    heads(1)
+    heads(2)
+    g5(DOWN)
+    heads(3)
+    heads(4)
+    heads(5)
     grad_out()
     r0(OUT)
     grad_wide(QKV, b.dqkv, 1 - core, b.away[0])
@@ -633,50 +700,51 @@
     grad_wide(QKV, b.dqkv, core, b.total[0])
     r1(QKV)
     ready(UP)
-    for t in range(6):
-        hidden(t)
-        if t == 2:
-            r2(OUT)
-    for t in range(6):
+    hidden(0)
+    hidden(1)
+    g6(DOWN)
+    hidden(2)
+    hidden(3)
+    hidden(4)
+    hidden(5)
+    r2(OUT)
+    for t in range(4):
         grad_down(t)
     r0(DOWN)
     r2(QKV)
+    e1()
     turn_xn2()
     ready(DOWN)
-    r1(DOWN)
     for t in range(6):
         hidden_back(t)
     grad_wide(UP, b.dh, 1 - core, b.away[2])
     r0(UP)
     grad_wide(UP, b.dh, core, b.total[2])
     r1(UP)
+    e2()
     r3(OUT)
     r3(QKV)
-    r2(DOWN)
     back_one()
     r2(UP)
-    r4(OUT)
-    r4(QKV)
     back_two()
     small_send(0)
-    r3(DOWN)
     z1(0)
+    e3()
+    r1(DOWN)
     small_take(0)
     r3(UP)
-    r4(DOWN)
+    z2(0)
+    small_take(1)
+    r3(DOWN)
+    z1(1)
     finish_forward()
-    small_take(1)
-    z2(0)
-    r4(UP)
-    z1(1)
     small_take(2)
-    z1(2)
+    e4()
+    z2(1)
     z3(0)
-    z2(1)
-    z2(2)
     small_take(3)
+    e5()
     z3(1)
-    z3(2)
     for copy in finals:
         copy.wait()
     for copy in started:

time: 127 us -> 122 us (0.961)
  Pallas kernels: 123 us -> 118 us
    pallas_call x1, Pallas kernels: 121 us -> 115 us  [per_device(): pl.pallas_call(kernel, out_shape=shapes + [jax.ShapeDtypeStruct((16, WIDE...]
where the time goes in v3:
time: 122 us; the launch traced here: 121 us
  Pallas kernels  118 us (97%)
  local copies, waits for them, and re-layouts  2.62 us (2%)
    pallas_call x1, Pallas kernels, per_device(): pl.pallas_call(kernel, out_shape=shapes + [jax.ShapeDtypeStruct((16, WIDE...  115 us
    pallas_call x1, Pallas kernels, per_device(): pl.pallas_call(deliver, out_shape=shapes + [jax.ShapeDtypeStruct((1, size...  2.73 us

profile of v3, /device:TPU:1, one launch (start us, length us, event | category | flops | bytes accessed | tf_op | source)
XLA Modules:
  0.0 121.3 jit_solution(11878796446961430691)
XLA Ops:
  0.6 0.0 copy-start.10
  0.7 0.0 copy-start.6
  0.7 0.0 copy-start.7
  0.7 0.0 copy-start.8
  0.7 0.0 copy-start.9
  0.7 0.0 copy-start.3
  0.7 0.0 copy-start.4
  0.7 0.0 copy-start.5
  0.7 0.6 copy-done.10
  1.3 0.0 copy-done.6
  1.3 0.0 copy-done.7
  1.3 0.0 copy-done.8
  1.4 0.0 copy-done.9
  1.4 0.0 copy-done.3
  1.4 0.0 copy-done.4
  1.4 0.0 copy-done.5
  1.4 0.0 copy-start
  1.4 0.0 copy-start.1
  1.4 0.0 copy-start.2
  1.4 0.1 concatenate.7
  1.5 0.6 copy-done
  2.1 0.0 copy-done.1
  2.1 0.0 copy-done.2
  2.1 0.6 stack.20.refs_3_
  2.7 0.6 broadcast_in_dim.10.refs_2_
  3.3 115.1 %shard_map.272 = (bf16[256,768]{1,0:T(8,128)(2,1)}, bf16[256,768]{1,0:T(8,128)(2,1)}, f32[24,2304]{1,0:T(8,128)}, f32[24,768]{1,0:T(8,128)}, f32[24,3072]{1,0:T(...) custom-call(bf16[256,768]{1,0:T(8,128)(2,1)} %refs_0_.1, bf16[256,768]{1,0:T(8,128)(2,1)} %refs_1_.1, ...), custom_call_target="tpu_custom_call" | custom-call | tf_op jit(solution)/shard_map/pallas_call | solution.py:801
  118.4 2.7 %shard_map.273 = (bf16[256,768]{1,0:T(8,128)(2,1)}, bf16[256,768]{1,0:T(8,128)(2,1)}, f32[24,2304]{1,0:T(8,128)}, f32[24,768]{1,0:T(8,128)}, f32[24,3072]{1,0:T(...) custom-call(bf16[256,768]{1,0:T(8,128)(2,1)} %get-tuple-element.35.r, ...), custom_call_target="tpu_custom_call" | custom-call | tf_op jit(solution)/shard_map/pallas_call | solution.py:811
  (1 shorter events, 0.0 us)
Async XLA Ops:
  0.6 0.7 copy-start.10
  0.7 0.7 copy-start.6
  0.7 0.7 copy-start.7
  0.7 0.7 copy-start.8
  0.7 0.7 copy-start.9
  0.7 0.7 copy-start.3
  0.7 0.7 copy-start.4
  0.7 0.7 copy-start.5
  1.4 0.7 copy-start
  1.4 0.7 copy-start.1
  1.4 0.7 copy-start.2
